TPU v7x, 256 devices: a whole 4x4x8 slice. The times are simulated.
256 devices in a mesh: dp: 64 (over y, z, core), width: 4 (over x).
Axes of the slice: x: 4, y: 4, z: 8, core: 2. Of those that a mesh axis runs over, the one named last changes fastest.
Arguments:
- queries: bfloat16 [8192, 3584], P('dp', 'width'), may hold values from -8 to 8
- codes: bfloat16 [8192, 3584], P('dp', 'width'), may hold values from -8 to 8
- pairing: int32 [64, 128], P('dp'), may hold values from 0 to 127, each once within a row
- neg_blocks: int32 [64, 4], replicated, may hold values from 0 to 63, as said below
- neg_count: int32 [64], replicated, may hold values from 1 to 4
Outputs:
- grad_queries: float32 [8192, 3584], P('dp', 'width')
- grad_codes: float32 [8192, 3584], P('dp', 'width')
Inputs may be any that keep to these rules, and one draw needn't show every extreme that they name: Row b of pairing orders 0 to 127, each once. `neg_blocks`: row b names 4 different blocks, none of them b.
All inputs are finite; a program needn't handle non-finite values.
Results may differ from a plain program's by a relative error of at most 0.0023.
Values may be sent and summed in bfloat16 or wider, within the bound.
No kernel may reach another device: no remote copies, remote signals or barrier semaphores. Data moves between devices by JAX's collectives and lax.ppermute only.
A program may use at most 64 MiB of HBM per device.

v0:
```python
import jax
import jax.numpy as jnp
from jax import lax
from jax.sharding import PartitionSpec as P

INV_TEMP = 50.0


def coefficients(scores, targets, valid):
    masked_scores = jnp.where(valid, scores, -jnp.inf)
    top = jnp.max(masked_scores, axis=1, keepdims=True)
    expo = jnp.where(valid, jnp.exp(masked_scores - top), 0.0)
    probs = expo / jnp.sum(expo, axis=1, keepdims=True)
    return (0.5 * (probs - targets)).astype(jnp.bfloat16)


def transposed_dot(left, right):
    return lax.dot_general(
        left, right, (((0,), (0,)), ((), ())), preferred_element_type=jnp.float32
    )


def local(queries, codes, pairing, neg_blocks, neg_count):
    rows, feats = queries.shape
    blocks = lax.axis_size("dp")
    piece = rows // blocks
    slots = neg_blocks.shape[1]
    me_block = lax.axis_index("dp")
    spread_q, spread_c = (
        lax.all_to_all(
            queries.reshape(blocks, piece, feats), "dp", split_axis=0, concat_axis=0, tiled=True
        ),
        lax.all_to_all(
            codes.reshape(blocks, piece, feats), "dp", split_axis=0, concat_axis=0, tiled=True
        ),
    )
    wanted = neg_blocks.T
    got_q, got_c = (
        lax.all_to_all(spread_q[wanted], "dp", split_axis=1, concat_axis=1, tiled=True),
        lax.all_to_all(spread_c[wanted], "dp", split_axis=1, concat_axis=1, tiled=True),
    )
    far_q = got_q.reshape(slots * rows, feats)
    far_c = got_c.reshape(slots * rows, feats)
    all_q = jnp.concatenate([queries, far_q], axis=0)
    all_c = jnp.concatenate([codes, far_c], axis=0)
    part_one = INV_TEMP * lax.dot_general(
        queries, all_c, (((1,), (1,)), ((), ())), preferred_element_type=jnp.float32
    )
    part_far = INV_TEMP * lax.dot_general(
        codes, far_q, (((1,), (1,)), ((), ())), preferred_element_type=jnp.float32
    )
    part_two = jnp.concatenate([part_one[:, :rows].T, part_far], axis=1)
    score_one, score_two = lax.psum((part_one, part_two), "width")
    count_me = lax.dynamic_index_in_dim(neg_count, me_block, 0, keepdims=False)
    columns = jnp.arange((slots + 1) * rows, dtype=jnp.int32)
    valid = (columns // rows <= count_me)[None, :]
    positions = pairing[0]
    target_one = (columns[None, :] == positions[:, None]).astype(jnp.float32)
    pos_ext = jnp.concatenate([positions, jnp.full((slots * rows,), -1, jnp.int32)])
    my_rows = jnp.arange(rows, dtype=jnp.int32)
    target_two = (pos_ext[None, :] == my_rows[:, None]).astype(jnp.float32)
    coef_one = coefficients(score_one, target_one, valid)
    coef_two = coefficients(score_two, target_two, valid)
    own_grad_q = INV_TEMP * (
        jnp.dot(coef_one, all_c, preferred_element_type=jnp.float32)
        + transposed_dot(coef_two[:, :rows], codes)
    )
    own_grad_c = INV_TEMP * (
        jnp.dot(coef_two, all_q, preferred_element_type=jnp.float32)
        + transposed_dot(coef_one[:, :rows], queries)
    )
    tail_two = coef_two[:, rows:].reshape(rows, slots, rows)
    tail_one = coef_one[:, rows:].reshape(rows, slots, rows)
    far_grad_q = (
        INV_TEMP * jnp.einsum("jrn,jd->rnd", tail_two, codes, preferred_element_type=jnp.float32)
    ).astype(jnp.bfloat16)
    far_grad_c = (
        INV_TEMP * jnp.einsum("jrn,jd->rnd", tail_one, queries, preferred_element_type=jnp.float32)
    ).astype(jnp.bfloat16)
    back_q, back_c = (
        lax.all_to_all(
            far_grad_q.reshape(slots, blocks, piece, feats),
            "dp",
            split_axis=1,
            concat_axis=1,
            tiled=True,
        ),
        lax.all_to_all(
            far_grad_c.reshape(slots, blocks, piece, feats),
            "dp",
            split_axis=1,
            concat_axis=1,
            tiled=True,
        ),
    )
    block_ids = jnp.arange(blocks, dtype=jnp.int32)
    live = jnp.arange(slots, dtype=jnp.int32)[:, None] < neg_count[None, :]
    routing = ((wanted[None, :, :] == block_ids[:, None, None]) & live[None, :, :]).astype(
        jnp.bfloat16
    )
    routing = routing.reshape(blocks, slots * blocks)
    summed_q = jnp.dot(
        routing, back_q.reshape(slots * blocks, piece * feats), preferred_element_type=jnp.float32
    )
    summed_c = jnp.dot(
        routing, back_c.reshape(slots * blocks, piece * feats), preferred_element_type=jnp.float32
    )
    home_q, home_c = (
        lax.all_to_all(
            summed_q.reshape(blocks, piece, feats).astype(jnp.bfloat16),
            "dp",
            split_axis=0,
            concat_axis=0,
            tiled=True,
        ).astype(jnp.float32),
        lax.all_to_all(
            summed_c.reshape(blocks, piece, feats).astype(jnp.bfloat16),
            "dp",
            split_axis=0,
            concat_axis=0,
            tiled=True,
        ).astype(jnp.float32),
    )
    grad_queries = own_grad_q + home_q.reshape(rows, feats)
    grad_codes = own_grad_c + home_c.reshape(rows, feats)
    return (grad_queries, grad_codes)


def solution(mesh):
    in_specs = (P("dp", "width"), P("dp", "width"), P("dp", None), P(), P())
    out_specs = (P("dp", "width"), P("dp", "width"))
    return jax.shard_map(local, mesh=mesh, in_specs=in_specs, out_specs=out_specs, check_vma=False)
```

profile of v0, /device:TPU:24, one launch (start us, length us, event | category | flops | bytes accessed | tf_op | source)
XLA Modules:
  0.0 290.6 jit_solution(13977148836275709560)
XLA Ops:
  7.2 1.7 reshape.97
  8.9 12.1 %all-to-all-start.2 = ((bf16[64,2,896]{2,1,0:T(2,128)(2,1)}), bf16[64,2,896]{2,1,0:T(2,128)(2,1)S(1)}, u32[]{:S(2)}, u32[]{:S(2)}) async-start(bf16[64,2,896]{2,1,0:T(2,128)(2,1)} %reshape.97), calls=%async_computation.2 | async-start | bytes 458752 | tf_op jit(solution)/shard_map/all_to_all | solution.py:30
  22.7 9.2 %all-to-all-done.2 = bf16[64,2,896]{2,1,0:T(2,128)(2,1)S(1)} async-done(((bf16[64,2,896]{2,1,0:T(2,128)(2,1)}), bf16[64,2,896]{2,1,0:T(2,128)(2,1)S(1)}, u32[]{:S(2)}, u32[]{:S(2)}) %all-to-all-start.2) | async-done | bytes 229408 | tf_op jit(solution)/shard_map/all_to_all | solution.py:30
  31.9 6.4 %all-to-all-start = ((bf16[64,2,896]{2,1,0:T(2,128)(2,1)}), bf16[64,2,896]{2,1,0:T(2,128)(2,1)S(1)}, u32[]{:S(2)}, u32[]{:S(2)}) async-start(bf16[64,2,896]{2,1,0:T(2,128)(2,1)} %reshape.95), calls=%async_computation | async-start | bytes 458752 | tf_op jit(solution)/shard_map/all_to_all | solution.py:33
  38.4 2.5 gather_fusion.1
  42.5 6.7 %all-to-all-done = bf16[64,2,896]{2,1,0:T(2,128)(2,1)S(1)} async-done(((bf16[64,2,896]{2,1,0:T(2,128)(2,1)}), bf16[64,2,896]{2,1,0:T(2,128)(2,1)S(1)}, u32[]{:S(2)}, u32[]{:S(2)}) %all-to-all-start) | async-done | bytes 229408 | tf_op jit(solution)/shard_map/all_to_all | solution.py:33
  49.2 6.4 %all-to-all-start.3 = ((bf16[4,64,2,896]{3,2,0,1:T(2,128)(2,1)}), bf16[4,64,2,896]{3,2,0,1:T(2,128)(2,1)S(1)}, u32[]{:S(2)}, u32[]{:S(2)}) async-start(bf16[4,64,2,896]{3,2,0,1:T(2,128)(2,1)} %copy.43), calls=%async_computation.3 | async-start | bytes 1835008 | tf_op jit(solution)/shard_map/all_to_all | solution.py:39
  55.7 2.5 gather_fusion
  59.8 20.0 %all-to-all-done.3 = bf16[4,64,2,896]{3,2,0,1:T(2,128)(2,1)S(1)} async-done(((bf16[4,64,2,896]{3,2,0,1:T(2,128)(2,1)}), bf16[4,64,2,896]{3,2,0,1:T(2,128)(2,1)S(1)}, u32[]{:S(2)}, u32[]{:S(2)}) %all-to-all-start.3) | async-done | bytes 917536 | tf_op jit(solution)/shard_map/all_to_all | solution.py:39
  79.8 8.0 %all-to-all-start.1 = ((bf16[4,64,2,896]{3,2,0,1:T(2,128)(2,1)}), bf16[4,64,2,896]{3,2,0,1:T(2,128)(2,1)}, u32[]{:S(2)}, u32[]{:S(2)}) async-start(bf16[4,64,2,896]{3,2,0,1:T(2,128)(2,1)} %copy.40), calls=%async_computation.1 | async-start | bytes 1835008 | tf_op jit(solution)/shard_map/all_to_all | solution.py:40
  89.6 2.5 reshape.98
  93.2 18.7 %all-to-all-done.1 = bf16[4,64,2,896]{3,2,0,1:T(2,128)(2,1)} async-done(((bf16[4,64,2,896]{3,2,0,1:T(2,128)(2,1)}), bf16[4,64,2,896]{3,2,0,1:T(2,128)(2,1)}, u32[]{:S(2)}, u32[]{:S(2)}) %all-to-all-start.1) | async-done | bytes 917536 | tf_op jit(solution)/shard_map/all_to_all | solution.py:40
  111.9 2.8 copy.41
  114.7 2.5 reshape.96
  121.0 46.2 %all-reduce.4.cloned.1.call-done = (f32[128,640]{1,0:T(8,128)}, f32[128,640]{1,0:T(8,128)}) async-done(((f32[128,640]{1,0:T(8,128)}, f32[128,640]{1,0:T(8,128)}), (f32[128,640]{1,0:T(8,128)}, f32[128,640]{1,0:T(8,128)})) %all-reduce.4.cloned.1.call-update) | async-done | bytes 655376 | tf_op jit(solution)/shard_map/psum | solution.py:53
  174.7 2.8 copy.48
  177.5 10.7 %all-to-all-start.4 = ((bf16[4,64,2,896]{3,2,0,1:T(2,128)(2,1)}), bf16[4,64,2,896]{3,2,0,1:T(2,128)(2,1)S(1)}, u32[]{:S(2)}, u32[]{:S(2)}) async-start(bf16[4,64,2,896]{3,2,0,1:T(2,128)(2,1)} %copy.48), calls=%async_computation.4 | async-start | bytes 1835008 | tf_op jit(solution)/shard_map/all_to_all | solution.py:81
  191.5 2.2 multiply_convert_fusion
  193.7 3.1 %reshape.105 = bf16[4,64,2,896]{3,2,1,0:T(2,128)(2,1)} reshape(bf16[4,128,896]{2,1,0:T(8,128)(2,1)} %multiply_convert_fusion) | data formatting | bytes 1835008 | tf_op jit(solution)/shard_map/reshape | solution.py:89
  196.8 2.7 copy.53
  199.5 12.9 %all-to-all-done.4 = bf16[4,64,2,896]{3,2,0,1:T(2,128)(2,1)S(1)} async-done(((bf16[4,64,2,896]{3,2,0,1:T(2,128)(2,1)}), bf16[4,64,2,896]{3,2,0,1:T(2,128)(2,1)S(1)}, u32[]{:S(2)}, u32[]{:S(2)}) %all-to-all-start.4) | async-done | bytes 917536 | tf_op jit(solution)/shard_map/all_to_all | solution.py:81
  213.4 7.8 %all-to-all-start.6 = ((bf16[4,64,2,896]{3,2,0,1:T(2,128)(2,1)}), bf16[4,64,2,896]{3,2,0,1:T(2,128)(2,1)S(1)}, u32[]{:S(2)}, u32[]{:S(2)}) async-start(bf16[4,64,2,896]{3,2,0,1:T(2,128)(2,1)} %copy.53), calls=%async_computation.6 | async-start | bytes 1835008 | tf_op jit(solution)/shard_map/all_to_all | solution.py:88
  221.4 1.8 copy.49
  224.3 2.2 copy.50
  229.0 16.3 %all-to-all-done.6 = bf16[4,64,2,896]{3,2,0,1:T(2,128)(2,1)S(1)} async-done(((bf16[4,64,2,896]{3,2,0,1:T(2,128)(2,1)}), bf16[4,64,2,896]{3,2,0,1:T(2,128)(2,1)S(1)}, u32[]{:S(2)}, u32[]{:S(2)}) %all-to-all-start.6) | async-done | bytes 917536 | tf_op jit(solution)/shard_map/all_to_all | solution.py:88
  245.4 8.0 %all-to-all-start.5 = ((bf16[64,2,896]{2,1,0:T(2,128)(2,1)}), bf16[64,2,896]{2,1,0:T(2,128)(2,1)}, u32[]{:S(2)}, u32[]{:S(2)}) async-start(bf16[64,2,896]{2,1,0:T(2,128)(2,1)} %copy.51), calls=%async_computation.5 | async-start | bytes 458752 | tf_op jit(solution)/shard_map/all_to_all | solution.py:109
  253.3 1.8 fusion.19
  259.6 4.6 %all-to-all-done.5 = bf16[64,2,896]{2,1,0:T(2,128)(2,1)} async-done(((bf16[64,2,896]{2,1,0:T(2,128)(2,1)}), bf16[64,2,896]{2,1,0:T(2,128)(2,1)}, u32[]{:S(2)}, u32[]{:S(2)}) %all-to-all-start.5) | async-done | bytes 229408 | tf_op jit(solution)/shard_map/all_to_all | solution.py:109
  264.2 6.6 %all-to-all-start.7 = ((bf16[64,2,896]{2,1,0:T(2,128)(2,1)}), bf16[64,2,896]{2,1,0:T(2,128)(2,1)}, u32[]{:S(2)}, u32[]{:S(2)}) async-start(bf16[64,2,896]{2,1,0:T(2,128)(2,1)} %copy.56), calls=%async_computation.7 | async-start | bytes 458752 | tf_op jit(solution)/shard_map/all_to_all | solution.py:116
  271.8 1.8 reshape.110
  273.6 2.3 fusion.1
  275.8 5.8 %all-to-all-done.7 = bf16[64,2,896]{2,1,0:T(2,128)(2,1)} async-done(((bf16[64,2,896]{2,1,0:T(2,128)(2,1)}), bf16[64,2,896]{2,1,0:T(2,128)(2,1)}, u32[]{:S(2)}, u32[]{:S(2)}) %all-to-all-start.7) | async-done | bytes 229408 | tf_op jit(solution)/shard_map/all_to_all | solution.py:116
  (69 shorter events, 34.8 us)
Async XLA Ops:
  7.2 31.2 %copy-start.10 = (s32[64,4]{0,1:T(4,128)S(1)}, s32[64,4]{0,1:T(4,128)}, u32[]{:S(2)}) copy-start(s32[64,4]{0,1:T(4,128)} %param.8) | copy-start | bytes 3076
  8.9 23.0 %all-to-all-start.2 = ((bf16[64,2,896]{2,1,0:T(2,128)(2,1)}), bf16[64,2,896]{2,1,0:T(2,128)(2,1)S(1)}, u32[]{:S(2)}, u32[]{:S(2)}) async-start(bf16[64,2,896]{2,1,0:T(2,128)(2,1)} %reshape.97), calls=%async_computation.2 | async-start | bytes 458752 | tf_op jit(solution)/shard_map/all_to_all | solution.py:30
  31.9 17.3 %all-to-all-start = ((bf16[64,2,896]{2,1,0:T(2,128)(2,1)}), bf16[64,2,896]{2,1,0:T(2,128)(2,1)S(1)}, u32[]{:S(2)}, u32[]{:S(2)}) async-start(bf16[64,2,896]{2,1,0:T(2,128)(2,1)} %reshape.95), calls=%async_computation | async-start | bytes 458752 | tf_op jit(solution)/shard_map/all_to_all | solution.py:33
  49.2 30.6 %all-to-all-start.3 = ((bf16[4,64,2,896]{3,2,0,1:T(2,128)(2,1)}), bf16[4,64,2,896]{3,2,0,1:T(2,128)(2,1)S(1)}, u32[]{:S(2)}, u32[]{:S(2)}) async-start(bf16[4,64,2,896]{3,2,0,1:T(2,128)(2,1)} %copy.43), calls=%async_computation.3 | async-start | bytes 1835008 | tf_op jit(solution)/shard_map/all_to_all | solution.py:39
  59.8 28.2 %copy-start = (bf16[128,896]{1,0:T(8,128)(2,1)S(1)}, bf16[128,896]{1,0:T(8,128)(2,1)}, u32[]{:S(2)}) copy-start(bf16[128,896]{1,0:T(8,128)(2,1)} %param.6) | copy-start | bytes 688132
  79.8 32.1 %all-to-all-start.1 = ((bf16[4,64,2,896]{3,2,0,1:T(2,128)(2,1)}), bf16[4,64,2,896]{3,2,0,1:T(2,128)(2,1)}, u32[]{:S(2)}, u32[]{:S(2)}) async-start(bf16[4,64,2,896]{3,2,0,1:T(2,128)(2,1)} %copy.40), calls=%async_computation.1 | async-start | bytes 1835008 | tf_op jit(solution)/shard_map/all_to_all | solution.py:40
  87.8 79.4 %all-reduce.4.cloned.1.call-start = ((), (), s32[]{:S(2)}) async-start(), calls=%async_computation.8 | async-start | bytes 1310720 | tf_op jit(solution)/shard_map/psum | solution.py:53
  117.1 0.9 copy-start.1
  118.1 0.9 copy-start.9
  118.5 1.2 copy-start.6
  118.6 1.3 copy-start.11
  118.6 1.3 copy-start.12
  167.2 2.4 copy-start.3
  167.2 2.5 copy-start.4
  170.7 0.7 copy-start.7
  177.5 34.9 %all-to-all-start.4 = ((bf16[4,64,2,896]{3,2,0,1:T(2,128)(2,1)}), bf16[4,64,2,896]{3,2,0,1:T(2,128)(2,1)S(1)}, u32[]{:S(2)}, u32[]{:S(2)}) async-start(bf16[4,64,2,896]{3,2,0,1:T(2,128)(2,1)} %copy.48), calls=%async_computation.4 | async-start | bytes 1835008 | tf_op jit(solution)/shard_map/all_to_all | solution.py:81
  212.4 1.0 copy-start.2
  213.4 32.0 %all-to-all-start.6 = ((bf16[4,64,2,896]{3,2,0,1:T(2,128)(2,1)}), bf16[4,64,2,896]{3,2,0,1:T(2,128)(2,1)S(1)}, u32[]{:S(2)}, u32[]{:S(2)}) async-start(bf16[4,64,2,896]{3,2,0,1:T(2,128)(2,1)} %copy.53), calls=%async_computation.6 | async-start | bytes 1835008 | tf_op jit(solution)/shard_map/all_to_all | solution.py:88
  245.4 18.8 %all-to-all-start.5 = ((bf16[64,2,896]{2,1,0:T(2,128)(2,1)}), bf16[64,2,896]{2,1,0:T(2,128)(2,1)}, u32[]{:S(2)}, u32[]{:S(2)}) async-start(bf16[64,2,896]{2,1,0:T(2,128)(2,1)} %copy.51), calls=%async_computation.5 | async-start | bytes 458752 | tf_op jit(solution)/shard_map/all_to_all | solution.py:109
  258.7 14.9 %copy-start.5 = (f32[128,896]{1,0:T(8,128)S(1)}, f32[128,896]{1,0:T(8,128)}, u32[]{:S(2)}) copy-start(f32[128,896]{1,0:T(8,128)} %fusion.19) | copy-start | bytes 1376260
  264.2 17.4 %all-to-all-start.7 = ((bf16[64,2,896]{2,1,0:T(2,128)(2,1)}), bf16[64,2,896]{2,1,0:T(2,128)(2,1)}, u32[]{:S(2)}, u32[]{:S(2)}) async-start(bf16[64,2,896]{2,1,0:T(2,128)(2,1)} %copy.56), calls=%async_computation.7 | async-start | bytes 458752 | tf_op jit(solution)/shard_map/all_to_all | solution.py:116
  273.6 9.1 %copy-start.8 = (bf16[128,640]{1,0:T(8,128)(2,1)S(1)}, bf16[128,640]{1,0:T(8,128)(2,1)}, u32[]{:S(2)}) copy-start(bf16[128,640]{1,0:T(8,128)(2,1)} %copy-done.7) | copy-start | bytes 491524
Sparse Core Ops, SparseCore 0:
  119.9 47.1 all-reduce.3
where the time goes:
time: 293 us; the launch traced here: 291 us
  waiting for transfers between devices  140 us (48%)
  starting transfers between devices  66.2 us (23%)
  local copies, waits for them, and re-layouts  51.6 us (18%)
  between operations  14.4 us (5%)
  matrix products  13.3 us (5%)
  other arithmetic  4.85 us (2%)
    psum x1, waiting for transfers between devices, local(): score_one, score_two = lax.psum((part_one, part_two), 'width')  46.2 us
    all_to_all x1, waiting for transfers between devices, local(): lax.all_to_all(spread_q[wanted], 'dp', split_axis=1, concat_axis=1, tiled...  20 us
    all_to_all x1, waiting for transfers between devices, local(): lax.all_to_all(spread_c[wanted], 'dp', split_axis=1, concat_axis=1, tiled...  18.7 us
    all_to_all x1, waiting for transfers between devices, local(): lax.all_to_all(far_grad_c.reshape(slots, blocks, piece, feats), 'dp', spl...  16.3 us
    all_to_all x1, waiting for transfers between devices, local(): lax.all_to_all(far_grad_q.reshape(slots, blocks, piece, feats), 'dp', spl...  12.9 us
    all_to_all x1, starting transfers between devices, local(): lax.all_to_all(queries.reshape(blocks, piece, feats), 'dp', split_axis=0,...  12.1 us
    all_to_all x1, starting transfers between devices, local(): lax.all_to_all(far_grad_q.reshape(slots, blocks, piece, feats), 'dp', spl...  10.7 us
    all_to_all x1, waiting for transfers between devices, local(): lax.all_to_all(queries.reshape(blocks, piece, feats), 'dp', split_axis=0,...  9.18 us
  transfers between devices with their start and end apart: 9, of which 9 were waited for; matrix products, arithmetic and copies ran while one was open for 16% of the time, Pallas kernels for 0%

commit v1 on v0

v1 whole, which is shorter than its diff:
```python
import functools

import jax
import jax.numpy as jnp
from jax import lax
from jax.experimental import pallas as pl
from jax.experimental.pallas import tpu as pltpu
from jax.sharding import Mesh, PartitionSpec as P

INV_TEMP = 50.0
NY, NZ, NC, NX = 4, 8, 2, 4
BLK = 128
SLOTS = 4
QUARTER = BLK // NX
HALF = BLK // 2
CAP_SMALL = 16
CAP_FULL = 80
LOWEST = -3.0e38
DP = ("y", "z", "c")
LIST_LEN = 88
F32 = jnp.float32
BF16 = jnp.bfloat16
VMEM = pltpu.VMEM
SMEM = pltpu.SMEM


def wrap(v, n):
    return v & (n - 1)


def spec_v():
    return pl.BlockSpec(memory_space=VMEM)


def spec_s():
    return pl.BlockSpec(memory_space=SMEM)


def list_kernel(neg_ref, count_ref, ent_ref):
    y, z, c, x = (lax.axis_index(name) for name in ("y", "z", "c", "x"))

    def push(k, e, j, take):
        ent_ref[0, k] = e
        ent_ref[1, k] = j
        return k + take.astype(jnp.int32)

    def first(e, k):
        b = ((y << 3) + wrap(z + e, NZ)) * NC + c
        count = count_ref[b]
        for r in range(SLOTS):
            n = neg_ref[b, r]
            take = (r < count) & (wrap(n >> 1, NZ) == z)
            k = push(k, e, 2 * wrap((n >> 4) - y, NY) + ((n & 1) ^ c), take)
        return k

    def second(j, k):
        b = ((wrap(y + (j >> 1), NY) << 3) + z) * NC + ((j & 1) ^ c)
        count = count_ref[b]
        for r in range(SLOTS):
            n = neg_ref[b, r]
            take = (r < count) & ((n >> 4) == y) & ((n & 1) == c)
            k = push(k, wrap((n >> 1) - z, NZ), j, take)
        return k

    n1 = lax.fori_loop(0, NZ, first, push(0, 0, 0, jnp.bool_(True)))
    n2 = lax.fori_loop(0, NY * NC, second, push(n1, 0, 0, jnp.bool_(True)))
    for i, v in enumerate((n1, n2, x, y, z, c)):
        ent_ref[2, i] = v


def build_list(neg_blocks, neg_count):
    return pl.pallas_call(
        list_kernel,
        out_shape=jax.ShapeDtypeStruct((3, LIST_LEN), jnp.int32),
        in_specs=[spec_s(), spec_s()],
        out_specs=spec_s(),
        name="block_list",
    )(neg_blocks, neg_count)


NQ, NCODE = 9, 8


def fill_blocks(q_refs, c_refs, qs, cs):
    own, l1, l2, l3, r1, r2, r3, r4, l4 = q_refs
    for e, ref in ((0, own), (1, l1), (2, l2), (3, l3), (7, r1), (6, r2), (5, r3)):
        qs[e] = ref[...]
    qs[4, :HALF] = r4[...]
    qs[4, HALF:] = l4[...]
    for j, ref in enumerate(c_refs):
        cs[j] = ref[...]


def dot_nt(a, b):
    return lax.dot_general(a, b, (((1,), (1,)), ((), ())), preferred_element_type=F32)


def dot_nn(a, b):
    return lax.dot_general(a, b, (((1,), (0,)), ((), ())), preferred_element_type=F32)


def dot_tn(a, b):
    return lax.dot_general(a, b, (((0,), (0,)), ((), ())), preferred_element_type=F32)


def quarter_starts(x):
    return [pl.multiple_of(wrap(x + d, NX) * QUARTER, QUARTER) for d in range(NX)]


def score_kernel(ent, *refs):
    q_refs, c_refs = refs[:NQ], refs[NQ : NQ + NCODE]
    outs = refs[NQ + NCODE : NQ + NCODE + NX]
    qs, cs, tile = refs[NQ + NCODE + NX :]
    fill_blocks(q_refs, c_refs, qs, cs)
    n1, n2 = ent[2, 0], ent[2, 1]
    starts = quarter_starts(ent[2, 2])

    def emit(k, s):
        tile[...] = s
        for out, start in zip(outs, starts):
            out[k] = tile[pl.ds(start, QUARTER), :]

    def first(k, _):
        emit(k, dot_nt(qs[ent[0, k]], cs[ent[1, k]]))
        return 0

    def second(k, _):
        emit(k, dot_nt(cs[ent[1, k]], qs[ent[0, k]]))
        return 0

    lax.fori_loop(0, n1, first, 0)
    lax.fori_loop(n1, n2, second, 0)


def partial_scores(cap, ent, q_parts, c_parts):
    feats = q_parts[0].shape[-1]
    return pl.pallas_call(
        score_kernel,
        out_shape=[jax.ShapeDtypeStruct((cap, QUARTER, BLK), F32)] * NX,
        in_specs=[spec_s()] + [spec_v()] * (NQ + NCODE),
        out_specs=[spec_v()] * NX,
        scratch_shapes=[
            VMEM((NZ, BLK, feats), BF16),
            VMEM((NY * NC, BLK, feats), BF16),
            VMEM((BLK, BLK), F32),
        ],
        compiler_params=pltpu.CompilerParams(vmem_limit_bytes=40 * 2**20),
        name="scores",
    )(ent, *q_parts, *c_parts)


def group_lane(ent, k, n1):
    y, z, c = ent[2, 3], ent[2, 4], ent[2, 5]
    e, j = ent[0, k], ent[1, k]
    first = wrap(z + e, NZ)
    second = NZ + 2 * wrap(y + (j >> 1), NY) + ((j & 1) ^ c)
    return jnp.where(k < n1, first, second)


def lanes_of(rows):
    return lax.broadcasted_iota(jnp.int32, (rows, BLK), 1)


def stats_kernel(ent, s0, s1, s2, s3, s_ref, st_ref, top, tot):
    n1, n2 = ent[2, 0], ent[2, 1]
    top[...] = jnp.full(top.shape, LOWEST, F32)
    tot[...] = jnp.zeros(tot.shape, F32)

    def first(k, _):
        s = INV_TEMP * ((s0[k] + s2[k]) + (s1[k] + s3[k]))
        s_ref[k] = s
        g = group_lane(ent, k, n1)
        top[g] = jnp.maximum(top[g], s)
        return 0

    lax.fori_loop(0, n2, first, 0)
    for g in range(2 * NZ):
        top[g] = jnp.broadcast_to(jnp.max(top[g], axis=1, keepdims=True), (QUARTER, BLK))

    def second(k, _):
        g = group_lane(ent, k, n1)
        tot[g] = tot[g] + jnp.exp(s_ref[k] - top[g])
        return 0

    lax.fori_loop(0, n2, second, 0)
    lane = lanes_of(QUARTER)
    m = jnp.full((QUARTER, BLK), LOWEST, F32)
    l = jnp.zeros((QUARTER, BLK), F32)
    for g in range(2 * NZ):
        m = jnp.where(lane == g, top[g], m)
        l = jnp.where(lane == g, jnp.sum(tot[g], axis=1, keepdims=True), l)
    st_ref[0] = m
    st_ref[1] = l


def local_stats(cap, ent, parts):
    return pl.pallas_call(
        stats_kernel,
        out_shape=[
            jax.ShapeDtypeStruct((cap, QUARTER, BLK), F32),
            jax.ShapeDtypeStruct((2, QUARTER, BLK), F32),
        ],
        in_specs=[spec_s()] + [spec_v()] * NX,
        out_specs=[spec_v()] * 2,
        scratch_shapes=[VMEM((2 * NZ, QUARTER, BLK), F32)] * 2,
        name="local_stats",
    )(ent, *parts)


def grad_kernel(ent, *refs):
    s_refs, st_refs, (prow, pcol) = refs[:NX], refs[NX : 2 * NX], refs[2 * NX : 2 * NX + 2]
    refs = refs[2 * NX + 2 :]
    q_refs, c_refs, refs = refs[:NQ], refs[NQ : NQ + NCODE], refs[NQ + NCODE :]
    own_q, own_c, pq, pc, po = refs[:5]
    qs, cs, acc_q, acc_c, st, tile = refs[5:]
    n1, n2 = ent[2, 0], ent[2, 1]
    fill_blocks(q_refs, c_refs, qs, cs)
    acc_q[...] = jnp.zeros(acc_q.shape, F32)
    acc_c[...] = jnp.zeros(acc_c.shape, F32)
    starts = quarter_starts(ent[2, 2])
    for ref, start in zip(st_refs, starts):
        st[:, pl.ds(start, QUARTER), :] = ref[...]
    lane = lanes_of(BLK)

    def probs(k):
        here = lane == group_lane(ent, k, n1)
        m = jnp.max(jnp.where(here, st[0], LOWEST), axis=1, keepdims=True)
        l = jnp.sum(jnp.where(here, st[1], 0.0), axis=1, keepdims=True)
        for ref, start in zip(s_refs, starts):
            tile[pl.ds(start, QUARTER), :] = ref[k]
        return jnp.exp(tile[...] - m) * (1.0 / l)

    def first(k, hit):
        e, j = ent[0, k], ent[1, k]
        g = (0.5 * (probs(k) - hit)).astype(BF16)
        acc_q[e] += dot_nn(g, cs[j])
        acc_c[j] += dot_tn(g, qs[e])

    def second(k, hit):
        e, j = ent[0, k], ent[1, k]
        g = (0.5 * (probs(k) - hit)).astype(BF16)
        acc_c[j] += dot_nn(g, qs[e])
        acc_q[e] += dot_tn(g, cs[j])

    def far(fn, k, _):
        fn(k, 0.0)
        return 0

    first(0, (pcol[...] == lane).astype(F32))
    lax.fori_loop(1, n1, functools.partial(far, first), 0)
    second(n1, (prow[...] == lax.broadcasted_iota(jnp.int32, (BLK, BLK), 0)).astype(F32))
    lax.fori_loop(n1 + 1, n2, functools.partial(far, second), 0)
    own_q[...] = INV_TEMP * acc_q[0]
    own_c[...] = INV_TEMP * acc_c[0]
    for e in range(1, NZ):
        pq[e - 1] = (INV_TEMP * acc_q[e]).astype(BF16)
    for d in range(NY):
        if d:
            pc[d - 1] = (INV_TEMP * acc_c[2 * d]).astype(BF16)
        po[d] = (INV_TEMP * acc_c[2 * d + 1]).astype(BF16)


def partial_grads(ent, scores, stats, pairing, q_parts, c_parts):
    feats = q_parts[0].shape[-1]
    return pl.pallas_call(
        grad_kernel,
        out_shape=[
            jax.ShapeDtypeStruct((BLK, feats), F32),
            jax.ShapeDtypeStruct((BLK, feats), F32),
            jax.ShapeDtypeStruct((NZ - 1, BLK, feats), BF16),
            jax.ShapeDtypeStruct((NY - 1, BLK, feats), BF16),
            jax.ShapeDtypeStruct((NY, BLK, feats), BF16),
        ],
        in_specs=[spec_s()] + [spec_v()] * (2 * NX + 2 + NQ + NCODE),
        out_specs=[spec_v()] * 5,
        scratch_shapes=[
            VMEM((NZ, BLK, feats), BF16),
            VMEM((NY * NC, BLK, feats), BF16),
            VMEM((NZ, BLK, feats), F32),
            VMEM((NY * NC, BLK, feats), F32),
            VMEM((2, BLK, BLK), F32),
            VMEM((BLK, BLK), F32),
        ],
        compiler_params=pltpu.CompilerParams(vmem_limit_bytes=52 * 2**20),
        name="grads",
    )(ent, *scores, *stats, pairing, pairing.reshape(BLK, 1), *q_parts, *c_parts)


def shift(value, axis, by):
    n = {"x": NX, "y": NY, "z": NZ, "c": NC}[axis]
    return lax.ppermute(value, axis, [(i, (i + by) % n) for i in range(n)])


def merge(a, b):
    m = jnp.maximum(a[0], b[0])
    return jnp.stack([m, a[1] * jnp.exp(a[0] - m) + b[1] * jnp.exp(b[0] - m)])


def merge_over_z(st):
    left, right = shift(st, "z", 1), shift(st, "z", -1)
    two = merge(left, st)
    three = merge(two, right)
    return merge(merge(three, shift(three, "z", 3)), shift(two, "z", -3))


def merge_over_yc(st):
    pair = merge(st, shift(st, "c", 1))
    return merge(
        merge(pair, shift(pair, "y", 2)), merge(shift(pair, "y", 1), shift(pair, "y", -1))
    )


def from_others(value, axis):
    return shift(value, axis, -1), shift(value, axis, 2), shift(value, axis, 1)


def gather_queries(q):
    r1, l1 = shift(q, "z", 1), shift(q, "z", -1)
    r2, l2 = shift(r1, "z", 1), shift(l1, "z", -1)
    r3, l3 = shift(r2, "z", 1), shift(l2, "z", -1)
    r4, l4 = shift(r3[:HALF], "z", 1), shift(l3[HALF:], "z", -1)
    return q, l1, l2, l3, r1, r2, r3, r4, l4


def gather_codes(codes):
    mine = (codes, *from_others(codes, "y"))
    return tuple(v for part in mine for v in (part, shift(part, "c", 1)))


def add(a, b):
    return (a.astype(F32) + b.astype(F32)).astype(BF16)


def reduce_queries(pq):
    r, l = shift(pq[3, :HALF], "z", 1), shift(pq[3, HALF:], "z", -1)
    r = jnp.concatenate([add(r, pq[2, :HALF]), pq[2, HALF:]], axis=0)
    l = jnp.concatenate([pq[4, :HALF], add(l, pq[4, HALF:])], axis=0)
    r, l = add(shift(r, "z", 1), pq[1]), add(shift(l, "z", -1), pq[5])
    r, l = add(shift(r, "z", 1), pq[0]), add(shift(l, "z", -1), pq[6])
    return shift(r, "z", 1), shift(l, "z", -1)


def reduce_codes(pc, po):
    other = shift(po, "c", 1)
    both = add(pc, other[1:])
    return other[0], shift(both[0], "y", 1), shift(both[1], "y", 2), shift(both[2], "y", -1)


def run(cap, queries, codes, pairing, neg_blocks, neg_count):
    ent = build_list(neg_blocks, neg_count)
    with jax.named_scope("gather"):
        c_parts = gather_codes(codes)
        q_parts = gather_queries(queries)
    o0, o1, o2, o3 = partial_scores(cap, ent, q_parts, c_parts)
    with jax.named_scope("scores_over_x"):
        parts = (o0, shift(o1, "x", 1), shift(o2, "x", 2), shift(o3, "x", -1))
    scores, st = local_stats(cap, ent, parts)
    with jax.named_scope("scores_to_x"):
        scores = (scores, *from_others(scores, "x"))
    with jax.named_scope("stats"):
        in_z = lax.broadcasted_iota(jnp.int32, st.shape, 2) < NZ
        st = jnp.where(in_z, merge_over_z(st), merge_over_yc(st))
        stats = (st, *from_others(st, "x"))
    own_q, own_c, pq, pc, po = partial_grads(ent, scores, stats, pairing, q_parts, c_parts)
    with jax.named_scope("reduce"):
        c0, c1, c2, c3 = reduce_codes(pc, po)
        qr, ql = reduce_queries(pq)
    grad_queries = own_q + (qr.astype(F32) + ql.astype(F32))
    grad_codes = own_c + ((c0.astype(F32) + c1.astype(F32)) + (c2.astype(F32) + c3.astype(F32)))
    return grad_queries, grad_codes


def longest_list(neg_blocks, neg_count):
    blocks = neg_blocks.shape[0]
    b = jnp.arange(blocks, dtype=jnp.int32)[:, None]
    live = jnp.arange(SLOTS, dtype=jnp.int32)[None, :] < neg_count[:, None]

    def tile(rows, cols):
        return (((rows >> 4) * NC + (rows & 1)) << 3) + ((cols >> 1) & 7)

    ids = jnp.arange(blocks, dtype=jnp.int32)[:, None, None]
    hits = (tile(b, neg_blocks)[None] == ids).astype(jnp.int32)
    hits += (tile(neg_blocks, b)[None] == ids).astype(jnp.int32)
    return jnp.max(jnp.sum(jnp.where(live[None], hits, 0), axis=(1, 2))) + 2


def local(*args):
    short = run(CAP_SMALL, *args)
    again = (longest_list(*args[3:]) > CAP_SMALL).astype(jnp.int32)
    return lax.while_loop(
        lambda state: state[0] > 0,
        lambda state: (jnp.int32(0), run(CAP_FULL, *args)),
        (again, short),
    )[1]


def solution(mesh):
    grid = Mesh(mesh.devices.reshape(NY, NZ, NC, NX), ("y", "z", "c", "x"))
    in_specs = (P(DP, "x"), P(DP, "x"), P(DP, None), P(), P())
    out_specs = (P(DP, "x"), P(DP, "x"))
    return jax.shard_map(local, mesh=grid, in_specs=in_specs, out_specs=out_specs, check_vma=False)
```

time: 293 us -> 148 us (0.51)
  waiting for transfers between devices: 140 us -> 47.6 us
  local copies, waits for them, and re-layouts: 51.6 us -> 5.87 us
  Pallas kernels: 0 us -> 17.6 us
  matrix products: 13.3 us -> 0 us
  between operations: 14.4 us -> 1.58 us
    all_to_all x8 -> x0, waiting for transfers between devices: 94.1 us -> none  [the longest x1 20 us: local(): lax.all_to_all(spread_q[wanted], 'dp', split_axis=1, concat_axis=1, tiled...]
    ppermute x0 -> x44, starting transfers between devices: none -> 67.6 us  [shift(): return lax.ppermute(value, axis, [(i, (i + by) % n) for i in range(n)])]
    all_to_all x8 -> x0, starting transfers between devices: 66 us -> none  [the longest x1 12.1 us: local(): lax.all_to_all(queries.reshape(blocks, piece, feats), 'dp', split_axis=0,...]
    ppermute x0 -> x44, waiting for transfers between devices: none -> 47.6 us  [shift(): return lax.ppermute(value, axis, [(i, (i + by) % n) for i in range(n)])]
    psum x1 -> x0, waiting for transfers between devices: 46.2 us -> none  [local(): score_one, score_two = lax.psum((part_one, part_two), 'width')]
    reshape x12 -> x1, local copies, waits for them, and re-layouts: 23.4 us -> 0.11 us  [partial_grads(): pairing.reshape(BLK, 1)]
    pallas_call x0 -> x4, Pallas kernels: none -> 17.6 us  [the longest x1 8.79 us: partial_grads(): pl.pallas_call(grad_kernel, out_shape=[jax.ShapeDtypeStruct((BLK, feats),...]
    dot_general x10 -> x0, matrix products: 13.3 us -> none  [the longest x2 2.77 us: transposed_dot(): lax.dot_general(left, right, (((0,), (0,)), ((), ())), preferred_element_...]
  transfers between devices with their start and end apart: 9 -> 44, of which waited for: 9 -> 19; matrix products, arithmetic and copies ran while one was open for 16% -> 4% of each run, Pallas kernels for 0% -> 2%
where the time goes in v1:
time: 148 us; the launch traced here: 147 us
  starting transfers between devices  67.6 us (46%)
  waiting for transfers between devices  47.6 us (32%)
  Pallas kernels  17.6 us (12%)
  other arithmetic  6.56 us (4%)
  local copies, waits for them, and re-layouts  5.87 us (4%)
  between operations  1.58 us (1%)
    ppermute x44, starting transfers between devices, shift(): return lax.ppermute(value, axis, [(i, (i + by) % n) for i in range(n)])  67.6 us
    ppermute x44, waiting for transfers between devices, shift(): return lax.ppermute(value, axis, [(i, (i + by) % n) for i in range(n)])  47.6 us
    pallas_call x1, Pallas kernels, partial_grads(): pl.pallas_call(grad_kernel, out_shape=[jax.ShapeDtypeStruct((BLK, feats),...  8.79 us
    unnamed x49, local copies, waits for them, and re-layouts  4.45 us
    pallas_call x1, Pallas kernels, partial_scores(): pl.pallas_call(score_kernel, out_shape=[jax.ShapeDtypeStruct((cap, QUARTE...  3.99 us
    convert_element_type x4, other arithmetic, add(): return (a.astype(F32) + b.astype(F32)).astype(BF16)  3.2 us
  transfers between devices with their start and end apart: 44, of which 19 were waited for; matrix products, arithmetic and copies ran while one was open for 4% of the time, Pallas kernels for 2%

profile of v1, /device:TPU:24, one launch (start us, length us, event | category | flops | bytes accessed | tf_op | source)
XLA Modules:
  0.0 146.9 jit_solution(6515002005850206334)
XLA Ops:
  2.6 4.0 %collective-permute-start.44 = (bf16[128,896]{1,0:T(8,128)(2,1)}, bf16[128,896]{1,0:T(8,128)(2,1)S(1)}, u32[]{:S(2)}, u32[]{:S(2)}) collective-permute-start(bf16[128,896]{1,0:T(8,128)(2,1)} %refs_10_.1), channel_id=1, source_target_pairs={{0,56},{8,0},{16,8},{24,16},{32,24},{40,32},{48,40},{56,48},{1,57}... | collective-permute-start | bytes 688136 | tf_op jit(solution)/shard_map/gather/ppermute | solution.py:291
  6.7 5.7 %collective-permute-done.47.refs_4_.refs_14_ = bf16[128,896]{1,0:T(8,128)(2,1)S(1)} collective-permute-done((bf16[128,896]{1,0:T(8,128)(2,1)}, bf16[128,896]{1,0:T(8,128)(2,1)S(1)}, u32[]{:S(2)}, u32[]{:S(2)}) %collective-permute-start.47) | collective-permute-done | bytes 229408 | tf_op jit(solution)/shard_map/gather/ppermute | solution.py:291
  12.4 3.2 %collective-permute-start.45 = (bf16[128,896]{1,0:T(8,128)(2,1)S(1)}, bf16[128,896]{1,0:T(8,128)(2,1)S(1)}, u32[]{:S(2)}, u32[]{:S(2)}) collective-permute-start(bf16[128,896]{1,0:T(8,128)(2,1)S(1)} %collective-permute-done.44.refs_1_.refs_11_), channel_id=1, source_target_pairs={{0,56},{8,0},{16,8},{24,16},{32,24},{40,32},{48,40},{56,48},{1,57}... | collective-permute-start | bytes 688136 | tf_op jit(solution)/shard_map/gather/ppermute | solution.py:291
  17.3 2.2 %collective-permute-start.57 = (bf16[128,896]{1,0:T(8,128)(2,1)}, bf16[128,896]{1,0:T(8,128)(2,1)S(1)}, u32[]{:S(2)}, u32[]{:S(2)}) collective-permute-start(bf16[128,896]{1,0:T(8,128)(2,1)} %refs_19_.1), channel_id=1, source_target_pairs={{0,64},{64,128},{128,192},{192,0},{1,65},{65,129},{129,193},{193,1... | collective-permute-start | bytes 688136 | tf_op jit(solution)/shard_map/gather/ppermute | solution.py:291
  20.4 3.2 %collective-permute-start.46 = (bf16[128,896]{1,0:T(8,128)(2,1)S(1)}, bf16[128,896]{1,0:T(8,128)(2,1)S(1)}, u32[]{:S(2)}, u32[]{:S(2)}) collective-permute-start(bf16[128,896]{1,0:T(8,128)(2,1)S(1)} %collective-permute-done.45.refs_2_.refs_12_), channel_id=1, source_target_pairs={{0,56},{8,0},{16,8},{24,16},{32,24},{40,32},{48,40},{56,48},{1,57}... | collective-permute-start | bytes 688136 | tf_op jit(solution)/shard_map/gather/ppermute | solution.py:291
  23.6 4.6 %collective-permute-done.53.refs_11_.refs_21_ = bf16[128,896]{1,0:T(8,128)(2,1)S(1)} collective-permute-done((bf16[128,896]{1,0:T(8,128)(2,1)}, bf16[128,896]{1,0:T(8,128)(2,1)S(1)}, u32[]{:S(2)}, u32[]{:S(2)}) %collective-permute-start.53) | collective-permute-done | bytes 229408 | tf_op jit(solution)/shard_map/gather/ppermute | solution.py:291
  29.9 2.8 %collective-permute-start.51 = (bf16[64,896]{1,0:T(8,128)(2,1)S(1)}, bf16[64,896]{1,0:T(8,128)(2,1)S(1)}, u32[]{:S(2)}, u32[]{:S(2)}) collective-permute-start(bf16[64,896]{1,0:T(8,128)(2,1)S(1)} %slice.293), channel_id=1, source_target_pairs={{0,56},{8,0},{16,8},{24,16},{32,24},{40,32},{48,40},{56,48},{1,57}... | collective-permute-start | bytes 344072 | tf_op jit(solution)/shard_map/gather/ppermute | solution.py:291
  33.5 2.4 %block_list.3.ent = s32[3,88]{1,0:T(4,128)} custom-call(s32[64,4]{1,0:T(8,128)S(1)} %copy.14.neg_ref, s32[64]{0:T(128)} %count_ref.1), custom_call_target="tpu_custom_call" | custom-call | tf_op jit(solution)/shard_map/block_list/pallas_call | solution.py:72
  36.6 4.0 %scores.3 = (f32[16,32,128]{2,1,0:T(8,128)S(1)}, f32[16,32,128]{2,1,0:T(8,128)S(1)}, f32[16,32,128]{2,1,0:T(8,128)S(1)}, f32[16,32,128]{2,1,0:T(8,128)S(1)}) custom-call(s32[3,88]{1,0:T(4,128)S(1)} %copy-done.18, bf16[128,896]{1,0:T(8,128)(2,1)} %refs_10_.1, bf16[128,896]{1,0:T(8,128)(2,1)S(1)} %collective-permute-done.44.refs_1_.refs_11_, ...), custom_call_target="tpu_custom_call" | custom-call | tf_op jit(solution)/shard_map/scores/pallas_call | solution.py:137
  42.9 2.7 %collective-permute-start.60 = (f32[16,32,128]{2,1,0:T(8,128)S(1)}, f32[16,32,128]{2,1,0:T(8,128)S(1)}, u32[]{:S(2)}, u32[]{:S(2)}) collective-permute-start(f32[16,32,128]{2,1,0:T(8,128)S(1)} %get-tuple-element.66), channel_id=1, source_target_pairs={{0,2},{1,3},{2,0},{3,1},{4,6},{5,7},{6,4},{7,5},{8,10},{9,11},{10,... | collective-permute-start | bytes 786440 | tf_op jit(solution)/shard_map/scores_over_x/ppermute | solution.py:291
  47.1 4.5 %collective-permute-done.59.s1 = f32[16,32,128]{2,1,0:T(8,128)S(1)} collective-permute-done((f32[16,32,128]{2,1,0:T(8,128)S(1)}, f32[16,32,128]{2,1,0:T(8,128)S(1)}, u32[]{:S(2)}, u32[]{:S(2)}) %collective-permute-start.59) | collective-permute-done | bytes 262176 | tf_op jit(solution)/shard_map/scores_over_x/ppermute | solution.py:291
  51.5 3.7 %collective-permute-done.60.s2 = f32[16,32,128]{2,1,0:T(8,128)S(1)} collective-permute-done((f32[16,32,128]{2,1,0:T(8,128)S(1)}, f32[16,32,128]{2,1,0:T(8,128)S(1)}, u32[]{:S(2)}, u32[]{:S(2)}) %collective-permute-start.60) | collective-permute-done | bytes 262176 | tf_op jit(solution)/shard_map/scores_over_x/ppermute | solution.py:291
  56.0 2.5 %local_stats.3 = (f32[16,32,128]{2,1,0:T(8,128)}, f32[2,32,128]{2,1,0:T(8,128)}) custom-call(s32[3,88]{1,0:T(4,128)} %block_list.3.ent, f32[16,32,128]{2,1,0:T(8,128)} %copy-done.17, f32[16,32,128]{2,1,0:T(8,128)} %copy-done.36, f32[16,32,128]{2,1,0:T(8,128)} %copy-done.37, f32[16,32,128]{2,1,0:T(8,128)} %copy-done.38), custom_call_target="tpu_custom_call" | custom-call | tf_op jit(solution)/shard_map/local_stats/pallas_call | solution.py:197
  59.3 2.4 %collective-permute-start.66 = (f32[2,32,128]{2,1,0:T(8,128)}, f32[2,32,128]{2,1,0:T(8,128)S(1)}, u32[]{:S(2)}, u32[]{:S(2)}) collective-permute-start(f32[2,32,128]{2,1,0:T(8,128)} %get-tuple-element.69), channel_id=1, source_target_pairs={{0,56},{8,0},{16,8},{24,16},{32,24},{40,32},{48,40},{56,48},{1,57}... | collective-permute-start | bytes 98312 | tf_op jit(solution)/shard_map/stats/ppermute | solution.py:291
  61.8 2.4 %collective-permute-start.62 = (f32[16,32,128]{2,1,0:T(8,128)}, f32[16,32,128]{2,1,0:T(8,128)S(1)}, u32[]{:S(2)}, u32[]{:S(2)}) collective-permute-start(f32[16,32,128]{2,1,0:T(8,128)} %get-tuple-element.68.refs_0_), channel_id=1, source_target_pairs={{0,3},{1,0},{2,1},{3,2},{4,7},{5,4},{6,5},{7,6},{8,11},{9,8},{10,9... | collective-permute-start | bytes 786440 | tf_op jit(solution)/shard_map/scores_to_x/ppermute | solution.py:291
  64.9 4.5 %collective-permute-start.67 = (f32[2,32,128]{2,1,0:T(8,128)S(1)}, f32[2,32,128]{2,1,0:T(8,128)S(1)}, u32[]{:S(2)}, u32[]{:S(2)}) collective-permute-start(f32[2,32,128]{2,1,0:T(8,128)S(1)} %pad_maximum_fusion.7), channel_id=1, source_target_pairs={{0,24},{8,32},{16,40},{24,48},{32,56},{40,0},{48,8},{56,16},{1,25}... | collective-permute-start | bytes 98312 | tf_op jit(solution)/shard_map/stats/ppermute | solution.py:291
  71.3 2.7 %collective-permute-start.71 = (f32[2,32,128]{2,1,0:T(8,128)S(1)}, f32[2,32,128]{2,1,0:T(8,128)S(1)}, u32[]{:S(2)}, u32[]{:S(2)}) collective-permute-start(f32[2,32,128]{2,1,0:T(8,128)S(1)} %pad_maximum_fusion.9), channel_id=1, source_target_pairs={{0,64},{64,128},{128,192},{192,0},{1,65},{65,129},{129,193},{193,1... | collective-permute-start | bytes 98312 | tf_op jit(solution)/shard_map/stats/ppermute | solution.py:291
  75.4 2.4 %collective-permute-start.63 = (f32[16,32,128]{2,1,0:T(8,128)}, f32[16,32,128]{2,1,0:T(8,128)S(1)}, u32[]{:S(2)}, u32[]{:S(2)}) collective-permute-start(f32[16,32,128]{2,1,0:T(8,128)} %get-tuple-element.68.refs_0_), channel_id=1, source_target_pairs={{0,2},{1,3},{2,0},{3,1},{4,6},{5,7},{6,4},{7,5},{8,10},{9,11},{10,... | collective-permute-start | bytes 786440 | tf_op jit(solution)/shard_map/scores_to_x/ppermute | solution.py:291
  79.2 2.2 %collective-permute-start.73 = (f32[2,32,128]{2,1,0:T(8,128)S(1)}, f32[2,32,128]{2,1,0:T(8,128)S(1)}, u32[]{:S(2)}, u32[]{:S(2)}) collective-permute-start(f32[2,32,128]{2,1,0:T(8,128)S(1)} %maximum_select_fusion.1.refs_4_), channel_id=1, source_target_pairs={{0,3},{1,0},{2,1},{3,2},{4,7},{5,4},{6,5},{7,6},{8,11},{9,8},{10,9... | collective-permute-start | bytes 98312 | tf_op jit(solution)/shard_map/stats/ppermute | solution.py:291
  85.6 4.4 %collective-permute-done.74.refs_6_ = f32[2,32,128]{2,1,0:T(8,128)S(1)} collective-permute-done((f32[2,32,128]{2,1,0:T(8,128)S(1)}, f32[2,32,128]{2,1,0:T(8,128)S(1)}, u32[]{:S(2)}, u32[]{:S(2)}) %collective-permute-start.74) | collective-permute-done | bytes 32800 | tf_op jit(solution)/shard_map/stats/ppermute | solution.py:291
  91.7 8.8 %grads.3 = (f32[128,896]{1,0:T(8,128)}, f32[128,896]{1,0:T(8,128)}, bf16[7,128,896]{2,1,0:T(8,128)(2,1)}, bf16[3,128,896]{2,1,0:T(8,128)(2,1)}, bf16[4,128,896]{2,1,0:T(8,128)(2,1)}) custom-call(s32[3,88]{1,0:T(4,128)S(1)} %copy-done.19, f32[16,32,128]{2,1,0:T(8,128)} %get-tuple-element.68.refs_0_, f32[16,32,128]{2,1,0:T(8,128)} %copy-done.33, ...), custom_call_target="tpu_custom_call" | custom-call | tf_op jit(solution)/shard_map/grads/pallas_call | solution.py:265
  102.0 3.1 %collective-permute-start.80 = (bf16[64,896]{1,0:T(8,128)(2,1)S(1)}, bf16[64,896]{1,0:T(8,128)(2,1)S(1)}, u32[]{:S(2)}, u32[]{:S(2)}) collective-permute-start(bf16[64,896]{1,0:T(8,128)(2,1)S(1)} %get-tuple-element.153), channel_id=1, source_target_pairs={{0,56},{8,0},{16,8},{24,16},{32,24},{40,32},{48,40},{56,48},{1,57}... | collective-permute-start | bytes 344072 | tf_op jit(solution)/shard_map/reduce/ppermute | solution.py:291
  105.1 2.8 %collective-permute-done.76 = bf16[64,896]{1,0:T(8,128)(2,1)S(1)} collective-permute-done((bf16[64,896]{1,0:T(8,128)(2,1)S(1)}, bf16[64,896]{1,0:T(8,128)(2,1)S(1)}, u32[]{:S(2)}, u32[]{:S(2)}) %collective-permute-start.76) | collective-permute-done | bytes 114720 | tf_op jit(solution)/shard_map/reduce/ppermute | solution.py:291
  108.9 3.3 %collective-permute-start.81 = (bf16[128,896]{1,0:T(8,128)(2,1)S(1)}, bf16[128,896]{1,0:T(8,128)(2,1)S(1)}, u32[]{:S(2)}, u32[]{:S(2)}) collective-permute-start(bf16[128,896]{1,0:T(8,128)(2,1)S(1)} %pad_maximum_fusion.6), channel_id=1, source_target_pairs={{0,56},{8,0},{16,8},{24,16},{32,24},{40,32},{48,40},{56,48},{1,57}... | collective-permute-start | bytes 688136 | tf_op jit(solution)/shard_map/reduce/ppermute | solution.py:291
  112.4 3.5 %collective-permute-done.81 = bf16[128,896]{1,0:T(8,128)(2,1)S(1)} collective-permute-done((bf16[128,896]{1,0:T(8,128)(2,1)S(1)}, bf16[128,896]{1,0:T(8,128)(2,1)S(1)}, u32[]{:S(2)}, u32[]{:S(2)}) %collective-permute-start.81) | collective-permute-done | bytes 229408 | tf_op jit(solution)/shard_map/reduce/ppermute | solution.py:291
  115.9 3.6 %collective-permute-done.77 = bf16[128,896]{1,0:T(8,128)(2,1)S(1)} collective-permute-done((bf16[128,896]{1,0:T(8,128)(2,1)S(1)}, bf16[128,896]{1,0:T(8,128)(2,1)S(1)}, u32[]{:S(2)}, u32[]{:S(2)}) %collective-permute-start.77) | collective-permute-done | bytes 229408 | tf_op jit(solution)/shard_map/reduce/ppermute | solution.py:291
  120.4 3.2 %collective-permute-start.82 = (bf16[128,896]{1,0:T(8,128)(2,1)}, bf16[128,896]{1,0:T(8,128)(2,1)}, u32[]{:S(2)}, u32[]{:S(2)}) collective-permute-start(bf16[128,896]{1,0:T(8,128)(2,1)} %get-tuple-element.149), channel_id=1, source_target_pairs={{0,56},{8,0},{16,8},{24,16},{32,24},{40,32},{48,40},{56,48},{1,57}... | collective-permute-start | bytes 688136 | tf_op jit(solution)/shard_map/reduce/ppermute | solution.py:291
  124.9 3.6 %collective-permute-done.78 = bf16[128,896]{1,0:T(8,128)(2,1)} collective-permute-done((bf16[128,896]{1,0:T(8,128)(2,1)}, bf16[128,896]{1,0:T(8,128)(2,1)}, u32[]{:S(2)}, u32[]{:S(2)}) %collective-permute-start.78) | collective-permute-done | bytes 229408 | tf_op jit(solution)/shard_map/reduce/ppermute | solution.py:291
  129.7 3.2 %collective-permute-start.83 = (bf16[128,896]{1,0:T(8,128)(2,1)S(1)}, bf16[128,896]{1,0:T(8,128)(2,1)S(1)}, u32[]{:S(2)}, u32[]{:S(2)}) collective-permute-start(bf16[128,896]{1,0:T(8,128)(2,1)S(1)} %get-tuple-element.147), channel_id=1, source_target_pairs={{0,56},{8,0},{16,8},{24,16},{32,24},{40,32},{48,40},{56,48},{1,57}... | collective-permute-start | bytes 688136 | tf_op jit(solution)/shard_map/reduce/ppermute | solution.py:291
  133.7 5.0 %collective-permute-start.86 = (bf16[128,896]{1,0:T(8,128)(2,1)S(1)}, bf16[128,896]{1,0:T(8,128)(2,1)S(1)}, u32[]{:S(2)}, u32[]{:S(2)}) collective-permute-start(bf16[128,896]{1,0:T(8,128)(2,1)S(1)} %get-tuple-element.158), channel_id=1, source_target_pairs={{0,128},{64,192},{128,0},{192,64},{1,129},{65,193},{129,1},{193,65... | collective-permute-start | bytes 688136 | tf_op jit(solution)/shard_map/reduce/ppermute | solution.py:291
  140.7 2.1 %collective-permute-done.86 = bf16[128,896]{1,0:T(8,128)(2,1)S(1)} collective-permute-done((bf16[128,896]{1,0:T(8,128)(2,1)S(1)}, bf16[128,896]{1,0:T(8,128)(2,1)S(1)}, u32[]{:S(2)}, u32[]{:S(2)}) %collective-permute-start.86) | collective-permute-done | bytes 229408 | tf_op jit(solution)/shard_map/reduce/ppermute | solution.py:291
  142.7 3.2 %collective-permute-done.87 = bf16[128,896]{1,0:T(8,128)(2,1)S(1)} collective-permute-done((bf16[128,896]{1,0:T(8,128)(2,1)S(1)}, bf16[128,896]{1,0:T(8,128)(2,1)S(1)}, u32[]{:S(2)}, u32[]{:S(2)}) %collective-permute-start.87) | collective-permute-done | bytes 229408 | tf_op jit(solution)/shard_map/reduce/ppermute | solution.py:291
  (136 shorter events, 33.5 us)
Async XLA Ops:
  0.6 11.7 %collective-permute-start.47 = (bf16[128,896]{1,0:T(8,128)(2,1)}, bf16[128,896]{1,0:T(8,128)(2,1)S(1)}, u32[]{:S(2)}, u32[]{:S(2)}) collective-permute-start(bf16[128,896]{1,0:T(8,128)(2,1)} %refs_10_.1), channel_id=1, source_target_pairs={{0,8},{8,16},{16,24},{24,32},{32,40},{40,48},{48,56},{56,0},{1,9},... | collective-permute-start | bytes 688136 | tf_op jit(solution)/shard_map/gather/ppermute | solution.py:291
  2.6 9.8 %collective-permute-start.44 = (bf16[128,896]{1,0:T(8,128)(2,1)}, bf16[128,896]{1,0:T(8,128)(2,1)S(1)}, u32[]{:S(2)}, u32[]{:S(2)}) collective-permute-start(bf16[128,896]{1,0:T(8,128)(2,1)} %refs_10_.1), channel_id=1, source_target_pairs={{0,56},{8,0},{16,8},{24,16},{32,24},{40,32},{48,40},{56,48},{1,57}... | collective-permute-start | bytes 688136 | tf_op jit(solution)/shard_map/gather/ppermute | solution.py:291
  12.4 8.0 %collective-permute-start.48 = (bf16[128,896]{1,0:T(8,128)(2,1)S(1)}, bf16[128,896]{1,0:T(8,128)(2,1)S(1)}, u32[]{:S(2)}, u32[]{:S(2)}) collective-permute-start(bf16[128,896]{1,0:T(8,128)(2,1)S(1)} %collective-permute-done.47.refs_4_.refs_14_), channel_id=1, source_target_pairs={{0,8},{8,16},{16,24},{24,32},{32,40},{40,48},{48,56},{56,0},{1,9},... | collective-permute-start | bytes 688136 | tf_op jit(solution)/shard_map/gather/ppermute | solution.py:291
  12.4 8.0 %collective-permute-start.45 = (bf16[128,896]{1,0:T(8,128)(2,1)S(1)}, bf16[128,896]{1,0:T(8,128)(2,1)S(1)}, u32[]{:S(2)}, u32[]{:S(2)}) collective-permute-start(bf16[128,896]{1,0:T(8,128)(2,1)S(1)} %collective-permute-done.44.refs_1_.refs_11_), channel_id=1, source_target_pairs={{0,56},{8,0},{16,8},{24,16},{32,24},{40,32},{48,40},{56,48},{1,57}... | collective-permute-start | bytes 688136 | tf_op jit(solution)/shard_map/gather/ppermute | solution.py:291
  15.6 12.6 %collective-permute-start.53 = (bf16[128,896]{1,0:T(8,128)(2,1)}, bf16[128,896]{1,0:T(8,128)(2,1)S(1)}, u32[]{:S(2)}, u32[]{:S(2)}) collective-permute-start(bf16[128,896]{1,0:T(8,128)(2,1)} %refs_19_.1), channel_id=1, source_target_pairs={{0,192},{64,0},{128,64},{192,128},{1,193},{65,1},{129,65},{193,129... | collective-permute-start | bytes 688136 | tf_op jit(solution)/shard_map/gather/ppermute | solution.py:291
  16.4 11.8 %collective-permute-start.55 = (bf16[128,896]{1,0:T(8,128)(2,1)}, bf16[128,896]{1,0:T(8,128)(2,1)S(1)}, u32[]{:S(2)}, u32[]{:S(2)}) collective-permute-start(bf16[128,896]{1,0:T(8,128)(2,1)} %refs_19_.1), channel_id=1, source_target_pairs={{0,128},{64,192},{128,0},{192,64},{1,129},{65,193},{129,1},{193,65... | collective-permute-start | bytes 688136 | tf_op jit(solution)/shard_map/gather/ppermute | solution.py:291
  17.3 11.5 %collective-permute-start.57 = (bf16[128,896]{1,0:T(8,128)(2,1)}, bf16[128,896]{1,0:T(8,128)(2,1)S(1)}, u32[]{:S(2)}, u32[]{:S(2)}) collective-permute-start(bf16[128,896]{1,0:T(8,128)(2,1)} %refs_19_.1), channel_id=1, source_target_pairs={{0,64},{64,128},{128,192},{192,0},{1,65},{65,129},{129,193},{193,1... | collective-permute-start | bytes 688136 | tf_op jit(solution)/shard_map/gather/ppermute | solution.py:291
  20.4 8.4 %collective-permute-start.49 = (bf16[128,896]{1,0:T(8,128)(2,1)S(1)}, bf16[128,896]{1,0:T(8,128)(2,1)S(1)}, u32[]{:S(2)}, u32[]{:S(2)}) collective-permute-start(bf16[128,896]{1,0:T(8,128)(2,1)S(1)} %collective-permute-done.48.refs_5_.refs_15_), channel_id=1, source_target_pairs={{0,8},{8,16},{16,24},{24,32},{32,40},{40,48},{48,56},{56,0},{1,9},... | collective-permute-start | bytes 688136 | tf_op jit(solution)/shard_map/gather/ppermute | solution.py:291
  20.4 9.0 %collective-permute-start.46 = (bf16[128,896]{1,0:T(8,128)(2,1)S(1)}, bf16[128,896]{1,0:T(8,128)(2,1)S(1)}, u32[]{:S(2)}, u32[]{:S(2)}) collective-permute-start(bf16[128,896]{1,0:T(8,128)(2,1)S(1)} %collective-permute-done.45.refs_2_.refs_12_), channel_id=1, source_target_pairs={{0,56},{8,0},{16,8},{24,16},{32,24},{40,32},{48,40},{56,48},{1,57}... | collective-permute-start | bytes 688136 | tf_op jit(solution)/shard_map/gather/ppermute | solution.py:291
  28.2 7.6 %collective-permute-start.54 = (bf16[128,896]{1,0:T(8,128)(2,1)S(1)}, bf16[128,896]{1,0:T(8,128)(2,1)S(1)}, u32[]{:S(2)}, u32[]{:S(2)}) collective-permute-start(bf16[128,896]{1,0:T(8,128)(2,1)S(1)} %collective-permute-done.53.refs_11_.refs_21_), channel_id=1, source_target_pairs={{0,4},{4,0},{1,5},{5,1},{2,6},{6,2},{3,7},{7,3},{8,12},{12,8},{9,1... | collective-permute-start | bytes 688136 | tf_op jit(solution)/shard_map/gather/ppermute | solution.py:291
  28.8 7.0 %collective-permute-start.56 = (bf16[128,896]{1,0:T(8,128)(2,1)S(1)}, bf16[128,896]{1,0:T(8,128)(2,1)S(1)}, u32[]{:S(2)}, u32[]{:S(2)}) collective-permute-start(bf16[128,896]{1,0:T(8,128)(2,1)S(1)} %collective-permute-done.55.refs_13_.refs_23_), channel_id=1, source_target_pairs={{0,4},{4,0},{1,5},{5,1},{2,6},{6,2},{3,7},{7,3},{8,12},{12,8},{9,1... | collective-permute-start | bytes 688136 | tf_op jit(solution)/shard_map/gather/ppermute | solution.py:291
  28.8 7.0 %collective-permute-start.58 = (bf16[128,896]{1,0:T(8,128)(2,1)S(1)}, bf16[128,896]{1,0:T(8,128)(2,1)S(1)}, u32[]{:S(2)}, u32[]{:S(2)}) collective-permute-start(bf16[128,896]{1,0:T(8,128)(2,1)S(1)} %collective-permute-done.57.refs_15_.refs_25_), channel_id=1, source_target_pairs={{0,4},{4,0},{1,5},{5,1},{2,6},{6,2},{3,7},{7,3},{8,12},{12,8},{9,1... | collective-permute-start | bytes 688136 | tf_op jit(solution)/shard_map/gather/ppermute | solution.py:291
  41.4 10.1 %collective-permute-start.59 = (f32[16,32,128]{2,1,0:T(8,128)S(1)}, f32[16,32,128]{2,1,0:T(8,128)S(1)}, u32[]{:S(2)}, u32[]{:S(2)}) collective-permute-start(f32[16,32,128]{2,1,0:T(8,128)S(1)} %get-tuple-element.65), channel_id=1, source_target_pairs={{0,1},{1,2},{2,3},{3,0},{4,5},{5,6},{6,7},{7,4},{8,9},{9,10},{10,1... | collective-permute-start | bytes 786440 | tf_op jit(solution)/shard_map/scores_over_x/ppermute | solution.py:291
  42.9 12.4 %collective-permute-start.60 = (f32[16,32,128]{2,1,0:T(8,128)S(1)}, f32[16,32,128]{2,1,0:T(8,128)S(1)}, u32[]{:S(2)}, u32[]{:S(2)}) collective-permute-start(f32[16,32,128]{2,1,0:T(8,128)S(1)} %get-tuple-element.66), channel_id=1, source_target_pairs={{0,2},{1,3},{2,0},{3,1},{4,6},{5,7},{6,4},{7,5},{8,10},{9,11},{10,... | collective-permute-start | bytes 786440 | tf_op jit(solution)/shard_map/scores_over_x/ppermute | solution.py:291
  45.6 9.6 %collective-permute-start.61 = (f32[16,32,128]{2,1,0:T(8,128)S(1)}, f32[16,32,128]{2,1,0:T(8,128)S(1)}, u32[]{:S(2)}, u32[]{:S(2)}) collective-permute-start(f32[16,32,128]{2,1,0:T(8,128)S(1)} %get-tuple-element.67), channel_id=1, source_target_pairs={{0,3},{1,0},{2,1},{3,2},{4,7},{5,4},{6,5},{7,6},{8,11},{9,8},{10,9... | collective-permute-start | bytes 786440 | tf_op jit(solution)/shard_map/scores_over_x/ppermute | solution.py:291
  61.8 28.4 %collective-permute-start.62 = (f32[16,32,128]{2,1,0:T(8,128)}, f32[16,32,128]{2,1,0:T(8,128)S(1)}, u32[]{:S(2)}, u32[]{:S(2)}) collective-permute-start(f32[16,32,128]{2,1,0:T(8,128)} %get-tuple-element.68.refs_0_), channel_id=1, source_target_pairs={{0,3},{1,0},{2,1},{3,2},{4,7},{5,4},{6,5},{7,6},{8,11},{9,8},{10,9... | collective-permute-start | bytes 786440 | tf_op jit(solution)/shard_map/scores_to_x/ppermute | solution.py:291
  64.9 9.1 %collective-permute-start.67 = (f32[2,32,128]{2,1,0:T(8,128)S(1)}, f32[2,32,128]{2,1,0:T(8,128)S(1)}, u32[]{:S(2)}, u32[]{:S(2)}) collective-permute-start(f32[2,32,128]{2,1,0:T(8,128)S(1)} %pad_maximum_fusion.7), channel_id=1, source_target_pairs={{0,24},{8,32},{16,40},{24,48},{32,56},{40,0},{48,8},{56,16},{1,25}... | collective-permute-start | bytes 98312 | tf_op jit(solution)/shard_map/stats/ppermute | solution.py:291
  70.0 7.8 %collective-permute-start.70 = (f32[2,32,128]{2,1,0:T(8,128)S(1)}, f32[2,32,128]{2,1,0:T(8,128)S(1)}, u32[]{:S(2)}, u32[]{:S(2)}) collective-permute-start(f32[2,32,128]{2,1,0:T(8,128)S(1)} %pad_maximum_fusion.9), channel_id=1, source_target_pairs={{0,128},{64,192},{128,0},{192,64},{1,129},{65,193},{129,1},{193,65... | collective-permute-start | bytes 98312 | tf_op jit(solution)/shard_map/stats/ppermute | solution.py:291
  71.3 7.2 %collective-permute-start.71 = (f32[2,32,128]{2,1,0:T(8,128)S(1)}, f32[2,32,128]{2,1,0:T(8,128)S(1)}, u32[]{:S(2)}, u32[]{:S(2)}) collective-permute-start(f32[2,32,128]{2,1,0:T(8,128)S(1)} %pad_maximum_fusion.9), channel_id=1, source_target_pairs={{0,64},{64,128},{128,192},{192,0},{1,65},{65,129},{129,193},{193,1... | collective-permute-start | bytes 98312 | tf_op jit(solution)/shard_map/stats/ppermute | solution.py:291
  75.4 14.8 %collective-permute-start.63 = (f32[16,32,128]{2,1,0:T(8,128)}, f32[16,32,128]{2,1,0:T(8,128)S(1)}, u32[]{:S(2)}, u32[]{:S(2)}) collective-permute-start(f32[16,32,128]{2,1,0:T(8,128)} %get-tuple-element.68.refs_0_), channel_id=1, source_target_pairs={{0,2},{1,3},{2,0},{3,1},{4,6},{5,7},{6,4},{7,5},{8,10},{9,11},{10,... | collective-permute-start | bytes 786440 | tf_op jit(solution)/shard_map/scores_to_x/ppermute | solution.py:291
  77.8 12.4 %collective-permute-start.64 = (f32[16,32,128]{2,1,0:T(8,128)}, f32[16,32,128]{2,1,0:T(8,128)S(1)}, u32[]{:S(2)}, u32[]{:S(2)}) collective-permute-start(f32[16,32,128]{2,1,0:T(8,128)} %get-tuple-element.68.refs_0_), channel_id=1, source_target_pairs={{0,1},{1,2},{2,3},{3,0},{4,5},{5,6},{6,7},{7,4},{8,9},{9,10},{10,1... | collective-permute-start | bytes 786440 | tf_op jit(solution)/shard_map/scores_to_x/ppermute | solution.py:291
  81.4 8.6 %collective-permute-start.74 = (f32[2,32,128]{2,1,0:T(8,128)S(1)}, f32[2,32,128]{2,1,0:T(8,128)S(1)}, u32[]{:S(2)}, u32[]{:S(2)}) collective-permute-start(f32[2,32,128]{2,1,0:T(8,128)S(1)} %maximum_select_fusion.1.refs_4_), channel_id=1, source_target_pairs={{0,2},{1,3},{2,0},{3,1},{4,6},{5,7},{6,4},{7,5},{8,10},{9,11},{10,... | collective-permute-start | bytes 98312 | tf_op jit(solution)/shard_map/stats/ppermute | solution.py:291
  108.9 7.1 %collective-permute-start.81 = (bf16[128,896]{1,0:T(8,128)(2,1)S(1)}, bf16[128,896]{1,0:T(8,128)(2,1)S(1)}, u32[]{:S(2)}, u32[]{:S(2)}) collective-permute-start(bf16[128,896]{1,0:T(8,128)(2,1)S(1)} %pad_maximum_fusion.6), channel_id=1, source_target_pairs={{0,56},{8,0},{16,8},{24,16},{32,24},{40,32},{48,40},{56,48},{1,57}... | collective-permute-start | bytes 688136 | tf_op jit(solution)/shard_map/reduce/ppermute | solution.py:291
  112.2 7.3 %collective-permute-start.77 = (bf16[128,896]{1,0:T(8,128)(2,1)S(1)}, bf16[128,896]{1,0:T(8,128)(2,1)S(1)}, u32[]{:S(2)}, u32[]{:S(2)}) collective-permute-start(bf16[128,896]{1,0:T(8,128)(2,1)S(1)} %pad_maximum_fusion.5), channel_id=1, source_target_pairs={{0,8},{8,16},{16,24},{24,32},{32,40},{40,48},{48,56},{56,0},{1,9},... | collective-permute-start | bytes 688136 | tf_op jit(solution)/shard_map/reduce/ppermute | solution.py:291
  112.3 20.7 %collective-permute-start.84 = (bf16[4,128,896]{2,1,0:T(8,128)(2,1)}, bf16[4,128,896]{2,1,0:T(8,128)(2,1)S(1)}, u32[]{:S(2)}, u32[]{:S(2)}) collective-permute-start(bf16[4,128,896]{2,1,0:T(8,128)(2,1)} %get-tuple-element.73), channel_id=1, source_target_pairs={{0,4},{4,0},{1,5},{5,1},{2,6},{6,2},{3,7},{7,3},{8,12},{12,8},{9,1... | collective-permute-start | bytes 2752520 | tf_op jit(solution)/shard_map/reduce/ppermute | solution.py:291
  120.4 8.1 %collective-permute-start.78 = (bf16[128,896]{1,0:T(8,128)(2,1)}, bf16[128,896]{1,0:T(8,128)(2,1)}, u32[]{:S(2)}, u32[]{:S(2)}) collective-permute-start(bf16[128,896]{1,0:T(8,128)(2,1)} %get-tuple-element.148), channel_id=1, source_target_pairs={{0,8},{8,16},{16,24},{24,32},{32,40},{40,48},{48,56},{56,0},{1,9},... | collective-permute-start | bytes 688136 | tf_op jit(solution)/shard_map/reduce/ppermute | solution.py:291
  120.4 8.1 %collective-permute-start.82 = (bf16[128,896]{1,0:T(8,128)(2,1)}, bf16[128,896]{1,0:T(8,128)(2,1)}, u32[]{:S(2)}, u32[]{:S(2)}) collective-permute-start(bf16[128,896]{1,0:T(8,128)(2,1)} %get-tuple-element.149), channel_id=1, source_target_pairs={{0,56},{8,0},{16,8},{24,16},{32,24},{40,32},{48,40},{56,48},{1,57}... | collective-permute-start | bytes 688136 | tf_op jit(solution)/shard_map/reduce/ppermute | solution.py:291
  129.7 9.1 %collective-permute-start.79 = (bf16[128,896]{1,0:T(8,128)(2,1)S(1)}, bf16[128,896]{1,0:T(8,128)(2,1)S(1)}, u32[]{:S(2)}, u32[]{:S(2)}) collective-permute-start(bf16[128,896]{1,0:T(8,128)(2,1)S(1)} %get-tuple-element.146), channel_id=1, source_target_pairs={{0,8},{8,16},{16,24},{24,32},{32,40},{40,48},{48,56},{56,0},{1,9},... | collective-permute-start | bytes 688136 | tf_op jit(solution)/shard_map/reduce/ppermute | solution.py:291
  129.7 9.0 %collective-permute-start.83 = (bf16[128,896]{1,0:T(8,128)(2,1)S(1)}, bf16[128,896]{1,0:T(8,128)(2,1)S(1)}, u32[]{:S(2)}, u32[]{:S(2)}) collective-permute-start(bf16[128,896]{1,0:T(8,128)(2,1)S(1)} %get-tuple-element.147), channel_id=1, source_target_pairs={{0,56},{8,0},{16,8},{24,16},{32,24},{40,32},{48,40},{56,48},{1,57}... | collective-permute-start | bytes 688136 | tf_op jit(solution)/shard_map/reduce/ppermute | solution.py:291
  133.2 7.4 %collective-permute-start.85 = (bf16[128,896]{1,0:T(8,128)(2,1)S(1)}, bf16[128,896]{1,0:T(8,128)(2,1)S(1)}, u32[]{:S(2)}, u32[]{:S(2)}) collective-permute-start(bf16[128,896]{1,0:T(8,128)(2,1)S(1)} %get-tuple-element.156), channel_id=1, source_target_pairs={{0,64},{64,128},{128,192},{192,0},{1,65},{65,129},{129,193},{193,1... | collective-permute-start | bytes 688136 | tf_op jit(solution)/shard_map/reduce/ppermute | solution.py:291
  133.7 9.0 %collective-permute-start.86 = (bf16[128,896]{1,0:T(8,128)(2,1)S(1)}, bf16[128,896]{1,0:T(8,128)(2,1)S(1)}, u32[]{:S(2)}, u32[]{:S(2)}) collective-permute-start(bf16[128,896]{1,0:T(8,128)(2,1)S(1)} %get-tuple-element.158), channel_id=1, source_target_pairs={{0,128},{64,192},{128,0},{192,64},{1,129},{65,193},{129,1},{193,65... | collective-permute-start | bytes 688136 | tf_op jit(solution)/shard_map/reduce/ppermute | solution.py:291
  138.7 7.2 %collective-permute-start.87 = (bf16[128,896]{1,0:T(8,128)(2,1)S(1)}, bf16[128,896]{1,0:T(8,128)(2,1)S(1)}, u32[]{:S(2)}, u32[]{:S(2)}) collective-permute-start(bf16[128,896]{1,0:T(8,128)(2,1)S(1)} %get-tuple-element.157), channel_id=1, source_target_pairs={{0,192},{64,0},{128,64},{192,128},{1,193},{65,1},{129,65},{193,129... | collective-permute-start | bytes 688136 | tf_op jit(solution)/shard_map/reduce/ppermute | solution.py:291
  (36 other events, 368.1 us)

commit v2 on v1

v2 whole, which is shorter than its diff:
```python
import functools

import jax
import jax.numpy as jnp
from jax import lax
from jax.experimental import pallas as pl
from jax.experimental.pallas import tpu as pltpu
from jax.sharding import Mesh, PartitionSpec as P

INV_TEMP = 50.0
NY, NZ, NC, NX = 4, 8, 2, 4
BLK = 128
SLOTS = 4
QUARTER = BLK // NX
HALF = BLK // 2
CAP_SMALL = 18
CAP_FULL = 80
LOWEST = -3.0e38
DP = ("y", "z", "c")
LIST_LEN = 88
GRANT_PER_SLOT = 5 * 2**14
F32 = jnp.float32
BF16 = jnp.bfloat16
VMEM = pltpu.VMEM
SMEM = pltpu.SMEM


def wrap(v, n):
    return v & (n - 1)


def grant(own, cap):
    return pltpu.CompilerParams(vmem_limit_bytes=own + GRANT_PER_SLOT * cap)


def spec_v():
    return pl.BlockSpec(memory_space=VMEM)


def spec_s():
    return pl.BlockSpec(memory_space=SMEM)


def list_kernel(neg_ref, count_ref, neg_v, count_v, ent_ref, over_ref):
    y, z, c, x = (lax.axis_index(name) for name in ("y", "z", "c", "x"))

    def push(k, e, j, take):
        ent_ref[0, k] = e
        ent_ref[1, k] = j
        return k + take.astype(jnp.int32)

    def first(e, k):
        b = ((y << 3) + wrap(z + e, NZ)) * NC + c
        count = count_ref[b]
        for r in range(SLOTS):
            n = neg_ref[r, b]
            take = (r < count) & (wrap(n >> 1, NZ) == z)
            k = push(k, e, 2 * wrap((n >> 4) - y, NY) + ((n & 1) ^ c), take)
        return k

    def second(j, k):
        b = ((wrap(y + (j >> 1), NY) << 3) + z) * NC + ((j & 1) ^ c)
        count = count_ref[b]
        for r in range(SLOTS):
            n = neg_ref[r, b]
            take = (r < count) & ((n >> 4) == y) & ((n & 1) == c)
            k = push(k, wrap((n >> 1) - z, NZ), j, take)
        return k

    n1 = lax.fori_loop(0, NZ, first, push(0, 0, 0, jnp.bool_(True)))
    n2 = lax.fori_loop(0, NY * NC, second, push(n1, 0, 0, jnp.bool_(True)))
    for i, v in enumerate((n1, n2, x, y, z, c)):
        ent_ref[2, i] = v
    blocks = count_v.shape[1]
    shape = (NZ, blocks)
    group = lax.broadcasted_iota(jnp.int32, shape, 0)
    b = lax.broadcasted_iota(jnp.int32, shape, 1)
    count = jnp.broadcast_to(count_v[...], shape)

    def rows_of(n):
        return ((n >> 4) << 1) + (n & 1)

    def cols_of(n):
        return wrap(n >> 1, NZ)

    def ones(mask):
        return jnp.where(mask, 1.0, 0.0)

    to_cols, to_rows = jnp.zeros(shape, F32), jnp.zeros(shape, F32)
    for r in range(SLOTS):
        n = jnp.broadcast_to(neg_v[pl.ds(r, 1), :], shape)
        to_cols += ones((cols_of(n) == group) & (r < count))
        to_rows += ones((rows_of(n) == group) & (r < count))
    tiles = dot_nt(ones(rows_of(b) == group), to_cols) + dot_nt(to_rows, ones(cols_of(b) == group))
    over_ref[0] = (jnp.max(tiles) + 2.0 > CAP_SMALL).astype(jnp.int32)


def build_list(neg_blocks, neg_count):
    neg = neg_blocks.T
    return pl.pallas_call(
        list_kernel,
        out_shape=[
            jax.ShapeDtypeStruct((3, LIST_LEN), jnp.int32),
            jax.ShapeDtypeStruct((1,), jnp.int32),
        ],
        in_specs=[spec_s(), spec_s(), spec_v(), spec_v()],
        out_specs=[spec_s(), spec_s()],
        compiler_params=grant(2 * 2**20, 0),
        name="block_list",
    )(neg, neg_count, neg, neg_count.reshape(1, -1))


NQ, NCODE = 9, 8


def fill_queries(q_refs, qs):
    own, l1, l2, l3, r1, r2, r3, r4, l4 = q_refs
    for e, ref in ((0, own), (1, l1), (2, l2), (3, l3), (7, r1), (6, r2), (5, r3)):
        qs[e] = ref[...]
    qs[4, :HALF] = r4[...]
    qs[4, HALF:] = l4[...]


def dot_nt(a, b):
    return lax.dot_general(a, b, (((1,), (1,)), ((), ())), preferred_element_type=F32)


def dot_nn(a, b):
    return lax.dot_general(a, b, (((1,), (0,)), ((), ())), preferred_element_type=F32)


def dot_tn(a, b):
    return lax.dot_general(a, b, (((0,), (0,)), ((), ())), preferred_element_type=F32)


def quarter_starts(x):
    return [pl.multiple_of(wrap(x + d, NX) * QUARTER, QUARTER) for d in range(NX)]


def score_kernel(ent, *refs):
    q_refs, c_refs = refs[:NQ], refs[NQ : NQ + NCODE]
    outs = refs[NQ + NCODE : NQ + NCODE + NX]
    qs, cs, tile = refs[NQ + NCODE + NX :]
    fill_queries(q_refs, qs)
    for j, ref in enumerate(c_refs):
        cs[j] = ref[...]
    n1, n2 = ent[2, 0], ent[2, 1]
    starts = quarter_starts(ent[2, 2])

    def emit(k, s):
        tile[...] = s
        for out, start in zip(outs, starts):
            out[k] = tile[pl.ds(start, QUARTER), :]

    def first(k, _):
        emit(k, dot_nt(qs[ent[0, k]], cs[ent[1, k]]))
        return 0

    def second(k, _):
        emit(k, dot_nt(cs[ent[1, k]], qs[ent[0, k]]))
        return 0

    lax.fori_loop(0, n1, first, 0)
    lax.fori_loop(n1, n2, second, 0)


def partial_scores(cap, ent, q_parts, c_parts):
    feats = q_parts[0].shape[-1]
    return pl.pallas_call(
        score_kernel,
        out_shape=[jax.ShapeDtypeStruct((cap, QUARTER, BLK), F32)] * NX,
        in_specs=[spec_s()] + [spec_v()] * (NQ + NCODE),
        out_specs=[spec_v()] * NX,
        scratch_shapes=[
            VMEM((NZ, BLK, feats), BF16),
            VMEM((NY * NC, BLK, feats), BF16),
            VMEM((BLK, BLK), F32),
        ],
        compiler_params=grant(8 * 2**20, cap),
        name="scores",
    )(ent, *q_parts, *c_parts)


def group_lane(ent, k, n1):
    y, z, c = ent[2, 3], ent[2, 4], ent[2, 5]
    e, j = ent[0, k], ent[1, k]
    first = wrap(z + e, NZ)
    second = NZ + 2 * wrap(y + (j >> 1), NY) + ((j & 1) ^ c)
    return jnp.where(k < n1, first, second)


def lanes_of(rows):
    return lax.broadcasted_iota(jnp.int32, (rows, BLK), 1)


def stats_kernel(ent, s0, s1, s2, s3, s_ref, st_ref, top, tot):
    n1, n2 = ent[2, 0], ent[2, 1]
    top[...] = jnp.full(top.shape, LOWEST, F32)
    tot[...] = jnp.zeros(tot.shape, F32)

    def first(k, _):
        s = INV_TEMP * ((s0[k] + s2[k]) + (s1[k] + s3[k]))
        s_ref[k] = s
        g = group_lane(ent, k, n1)
        top[g] = jnp.maximum(top[g], s)
        return 0

    lax.fori_loop(0, n2, first, 0)
    for g in range(2 * NZ):
        top[g] = jnp.broadcast_to(jnp.max(top[g], axis=1, keepdims=True), (QUARTER, BLK))

    def second(k, _):
        g = group_lane(ent, k, n1)
        tot[g] = tot[g] + jnp.exp(s_ref[k] - top[g])
        return 0

    lax.fori_loop(0, n2, second, 0)
    lane = lanes_of(QUARTER)
    m = jnp.full((QUARTER, BLK), LOWEST, F32)
    l = jnp.zeros((QUARTER, BLK), F32)
    for g in range(2 * NZ):
        m = jnp.where(lane == g, top[g], m)
        l = jnp.where(lane == g, jnp.sum(tot[g], axis=1, keepdims=True), l)
    st_ref[0] = m
    st_ref[1] = l


def local_stats(cap, ent, parts):
    return pl.pallas_call(
        stats_kernel,
        out_shape=[
            jax.ShapeDtypeStruct((cap, QUARTER, BLK), F32),
            jax.ShapeDtypeStruct((2, QUARTER, BLK), F32),
        ],
        in_specs=[spec_s()] + [spec_v()] * NX,
        out_specs=[spec_v()] * 2,
        scratch_shapes=[VMEM((2 * NZ, QUARTER, BLK), F32)] * 2,
        compiler_params=grant(2 * 2**20, cap),
        name="local_stats",
    )(ent, *parts)


def query_grad_kernel(ent, *refs):
    s_refs, st_refs, prow = refs[:NX], refs[NX : 2 * NX], refs[2 * NX]
    c_refs, refs = refs[2 * NX + 1 : 2 * NX + 1 + NCODE], refs[2 * NX + 1 + NCODE :]
    g_ref, own, p1, p2, p3, p4a, p4b, m1, m2, m3 = refs[:10]
    cs, acc, st, tile = refs[10:]
    n1, n2 = ent[2, 0], ent[2, 1]
    for j, ref in enumerate(c_refs):
        cs[j] = ref[...]
    acc[...] = jnp.zeros(acc.shape, F32)
    starts = quarter_starts(ent[2, 2])
    for ref, start in zip(st_refs, starts):
        st[:, pl.ds(start, QUARTER), :] = ref[...]
    lane = lanes_of(BLK)

    def coefs(k, hit):
        here = lane == group_lane(ent, k, n1)
        m = jnp.max(jnp.where(here, st[0], LOWEST), axis=1, keepdims=True)
        l = jnp.sum(jnp.where(here, st[1], 0.0), axis=1, keepdims=True)
        for ref, start in zip(s_refs, starts):
            tile[pl.ds(start, QUARTER), :] = ref[k]
        g = (0.5 * (jnp.exp(tile[...] - m) * (1.0 / l) - hit)).astype(BF16)
        g_ref[k] = g
        return g

    def first(k, hit):
        acc[ent[0, k]] += dot_nn(coefs(k, hit), cs[ent[1, k]])

    def second(k, hit):
        acc[ent[0, k]] += dot_tn(coefs(k, hit), cs[ent[1, k]])

    def far(fn, k, _):
        fn(k, 0.0)
        return 0

    hit = (prow[...] == lax.broadcasted_iota(jnp.int32, (BLK, BLK), 0)).astype(F32)
    first(0, hit.T)
    lax.fori_loop(1, n1, functools.partial(far, first), 0)
    second(n1, hit)
    lax.fori_loop(n1 + 1, n2, functools.partial(far, second), 0)
    own[...] = INV_TEMP * acc[0]
    for e, out in ((1, p1), (2, p2), (3, p3), (7, m1), (6, m2), (5, m3)):
        out[...] = (INV_TEMP * acc[e]).astype(BF16)
    p4a[...] = (INV_TEMP * acc[4, :HALF]).astype(BF16)
    p4b[...] = (INV_TEMP * acc[4, HALF:]).astype(BF16)


def query_grads(cap, ent, scores, stats, pairing, c_parts):
    feats = c_parts[0].shape[-1]
    part = jax.ShapeDtypeStruct((BLK, feats), BF16)
    half = jax.ShapeDtypeStruct((HALF, feats), BF16)
    return pl.pallas_call(
        query_grad_kernel,
        out_shape=[
            jax.ShapeDtypeStruct((cap, BLK, BLK), BF16),
            jax.ShapeDtypeStruct((BLK, feats), F32),
            *[part, part, part, half, half, part, part, part],
        ],
        in_specs=[spec_s()] + [spec_v()] * (2 * NX + 1 + NCODE),
        out_specs=[spec_v()] * 10,
        scratch_shapes=[
            VMEM((NY * NC, BLK, feats), BF16),
            VMEM((NZ, BLK, feats), F32),
            VMEM((2, BLK, BLK), F32),
            VMEM((BLK, BLK), F32),
        ],
        compiler_params=grant(10 * 2**20, cap),
        cost_estimate=pl.CostEstimate(flops=10**9, bytes_accessed=12 * 10**6, transcendentals=10**5),
        name="query_grads",
    )(ent, *scores, *stats, pairing, *c_parts)


def code_grad_kernel(ent, g_ref, *refs):
    q_refs, (own, pc1, pc2, pc3, po, qs, acc) = refs[:NQ], refs[NQ:]
    n1, n2 = ent[2, 0], ent[2, 1]
    fill_queries(q_refs, qs)
    acc[...] = jnp.zeros(acc.shape, F32)

    def first(k, _):
        acc[ent[1, k]] += dot_tn(g_ref[k], qs[ent[0, k]])
        return 0

    def second(k, _):
        acc[ent[1, k]] += dot_nn(g_ref[k], qs[ent[0, k]])
        return 0

    lax.fori_loop(0, n1, first, 0)
    lax.fori_loop(n1, n2, second, 0)
    own[...] = INV_TEMP * acc[0]
    for d, out in ((1, pc1), (2, pc2), (3, pc3)):
        out[...] = (INV_TEMP * acc[2 * d]).astype(BF16)
    for d in range(NY):
        po[d] = (INV_TEMP * acc[2 * d + 1]).astype(BF16)


def code_grads(ent, coefs, q_parts):
    feats = q_parts[0].shape[-1]
    part = jax.ShapeDtypeStruct((BLK, feats), BF16)
    return pl.pallas_call(
        code_grad_kernel,
        out_shape=[
            jax.ShapeDtypeStruct((BLK, feats), F32),
            *[part, part, part],
            jax.ShapeDtypeStruct((NY, BLK, feats), BF16),
        ],
        in_specs=[spec_s()] + [spec_v()] * (1 + NQ),
        out_specs=[spec_v()] * 5,
        scratch_shapes=[VMEM((NZ, BLK, feats), BF16), VMEM((NY * NC, BLK, feats), F32)],
        compiler_params=grant(10 * 2**20, coefs.shape[0]),
        cost_estimate=pl.CostEstimate(flops=10**9, bytes_accessed=12 * 10**6, transcendentals=0),
        name="code_grads",
    )(ent, coefs, *q_parts)


def shift(value, axis, by):
    n = {"x": NX, "y": NY, "z": NZ, "c": NC}[axis]
    return lax.ppermute(value, axis, [(i, (i + by) % n) for i in range(n)])


def merge(a, b):
    m = jnp.maximum(a[0], b[0])
    return m, a[1] * jnp.exp(a[0] - m) + b[1] * jnp.exp(b[0] - m)


def small_kernel(fn, name, out_shape, *args):
    def kernel(*refs):
        outs = fn(*(ref[...] for ref in refs[: len(args)]))
        for ref, out in zip(refs[len(args) :], outs):
            ref[...] = out

    return pl.pallas_call(
        kernel,
        out_shape=out_shape,
        in_specs=[spec_v()] * len(args),
        out_specs=[spec_v()] * len(out_shape),
        compiler_params=grant(4 * 2**20, 0),
        name=name,
    )(*args)


def near_stats(st, left, right, other):
    two = merge(left, st)
    return jnp.stack(two), jnp.stack(merge(two, right)), jnp.stack(merge(st, other))


def final_stats(three, pair, z1, z2, y1, y2, y3):
    over_z = merge(merge(three, z1), z2)
    over_yc = merge(merge(pair, y1), merge(y2, y3))
    first = lanes_of(QUARTER) < NZ
    return (jnp.stack([jnp.where(first, a, b) for a, b in zip(over_z, over_yc)]),)


def from_others(value, axis):
    return shift(value, axis, -1), shift(value, axis, 2), shift(value, axis, 1)


def gather(queries, codes, ent):
    r1, l1 = shift(queries, "z", 1), shift(queries, "z", -1)
    c_mine = (codes, *from_others(codes, "y"))
    c_parts = tuple(v for part in c_mine for v in (part, shift(part, "c", 1)))
    r1, l1, ent = lax.optimization_barrier((r1, l1, ent))
    r2, l2 = shift(r1, "z", 1), shift(l1, "z", -1)
    r3, l3 = shift(r2, "z", 1), shift(l2, "z", -1)
    r4, l4 = shift(r3[:HALF], "z", 1), shift(l3[HALF:], "z", -1)
    return (queries, l1, l2, l3, r1, r2, r3, r4, l4), c_parts, ent


def exchange(cap, scores, st):
    others = from_others(scores, "x")
    left, right, other = shift(st, "z", 1), shift(st, "z", -1), shift(st, "c", 1)
    like = jax.ShapeDtypeStruct(st.shape, F32)
    two, three, pair = small_kernel(near_stats, "near_stats", [like] * 3, st, left, right, other)
    z1, z2 = shift(three, "z", 3), shift(two, "z", -3)
    y1, y2, y3 = from_others(pair, "y")
    (st,) = small_kernel(final_stats, "final_stats", [like], three, pair, z1, z2, y1, y2, y3)
    return (scores, *others), (st, *from_others(st, "x"))


def total(*parts):
    out = parts[0].astype(F32)
    for p in parts[1:]:
        out = out + p.astype(F32)
    return out


def join_halves(b, d, r, l):
    r = jnp.concatenate([total(b, r[:HALF]).astype(BF16), r[HALF:]], axis=0)
    return r, jnp.concatenate([l[:HALF], total(d, l[HALF:]).astype(BF16)], axis=0)


def join(a, b, r, l):
    return total(a, r).astype(BF16), total(b, l).astype(BF16)


def join_codes(other, *parts):
    return [total(part, other[d + 1]).astype(BF16) for d, part in enumerate(parts)]


def reduce_queries(p1, p2, p3, p4a, p4b, m1, m2, m3):
    like = [jax.ShapeDtypeStruct(p1.shape, BF16)] * 2
    r, l = shift(p4a, "z", 1), shift(p4b, "z", -1)
    r, l = small_kernel(join_halves, "join_halves", like, r, l, p3, m3)
    for a, b in ((p2, m2), (p1, m1)):
        r, l = shift(r, "z", 1), shift(l, "z", -1)
        r, l = small_kernel(join, "join", like, r, l, a, b)
    return shift(r, "z", 1), shift(l, "z", -1)


def reduce_codes(po, *parts):
    like = [jax.ShapeDtypeStruct(parts[0].shape, BF16)] * 3
    other = shift(po, "c", 1)
    parts = small_kernel(join_codes, "join_codes", like, other, *parts)
    return other[0], *(shift(part, "y", d + 1) for d, part in enumerate(parts))


def run(cap, queries, codes, pairing, neg_blocks, neg_count):
    ent, over = build_list(neg_blocks, neg_count)
    with jax.named_scope("gather"):
        q_parts, c_parts, ent = gather(queries, codes, ent)
    o0, o1, o2, o3 = partial_scores(cap, ent, q_parts, c_parts)
    with jax.named_scope("scores_over_x"):
        parts = (o0, shift(o1, "x", 1), shift(o2, "x", 2), shift(o3, "x", -1))
    scores, st = local_stats(cap, ent, parts)
    with jax.named_scope("stats"):
        scores, stats = exchange(cap, scores, st)
    g, own_q, p1, p2, p3, p4a, p4b, m1, m2, m3 = query_grads(
        cap, ent, scores, stats, pairing, c_parts
    )
    own_c, pc1, pc2, pc3, po = code_grads(ent, g, q_parts)
    with jax.named_scope("reduce"):
        from_z = reduce_queries(p1, p2, p3, p4a, p4b, m1, m2, m3)
        from_yc = reduce_codes(po, pc1, pc2, pc3)
    return over, (total(own_q, *from_z), total(own_c, *from_yc))


def local(*args):
    over, short = run(CAP_SMALL, *args)
    return lax.while_loop(
        lambda state: state[0] > 0,
        lambda state: (jnp.int32(0), run(CAP_FULL, *args)[1]),
        (over[0], short),
    )[1]


def solution(mesh):
    grid = Mesh(mesh.devices.reshape(NY, NZ, NC, NX), ("y", "z", "c", "x"))
    in_specs = (P(DP, "x"), P(DP, "x"), P(DP, None), P(), P())
    out_specs = (P(DP, "x"), P(DP, "x"))
    return jax.shard_map(local, mesh=grid, in_specs=in_specs, out_specs=out_specs, check_vma=False)
```

time: 148 us -> 144 us (0.973); the launches traced: 147 us -> 144 us
  waiting for transfers between devices: 47.6 us -> 61.1 us
  Pallas kernels: 17.6 us -> 11.7 us
  local copies, waits for them, and re-layouts: 5.87 us -> 0.04 us
  other arithmetic: 6.56 us -> 1.73 us
    ppermute x44, waiting for transfers between devices: 47.6 us -> 61.1 us  [shift(): return lax.ppermute(value, axis, [(i, (i + by) % n) for i in range(n)])]
    unnamed x49 -> x6, local copies, waits for them, and re-layouts: 4.45 us -> 0.02 us
    convert_element_type x4 -> x0, other arithmetic: 3.2 us -> none  [add(): return (a.astype(F32) + b.astype(F32)).astype(BF16)]
    pallas_call x2 -> x9, Pallas kernels: 11.2 us -> 8.39 us  [the longest x1 3.24 us: query_grads(): pl.pallas_call(query_grad_kernel, out_shape=[jax.ShapeDtypeStruct((cap, B...]
    pallas_call x1, Pallas kernels: 3.99 us -> 2.3 us  [partial_scores(): pl.pallas_call(score_kernel, out_shape=[jax.ShapeDtypeStruct((cap, QUARTE...]
  transfers between devices with their start and end apart: 44 -> 44, of which waited for: 19 -> 27; matrix products, arithmetic and copies ran while one was open for 4% -> 1% of each run, Pallas kernels for 2% -> 2%
where the time goes in v2:
time: 144 us
  starting transfers between devices  68.1 us (47%)
  waiting for transfers between devices  61.1 us (42%)
  Pallas kernels  11.7 us (8%)
  other arithmetic  1.73 us (1%)
    ppermute x44, starting transfers between devices, shift(): return lax.ppermute(value, axis, [(i, (i + by) % n) for i in range(n)])  68.1 us
    ppermute x44, waiting for transfers between devices, shift(): return lax.ppermute(value, axis, [(i, (i + by) % n) for i in range(n)])  61.1 us
    pallas_call x1, Pallas kernels, query_grads(): pl.pallas_call(query_grad_kernel, out_shape=[jax.ShapeDtypeStruct((cap, B...  3.24 us
  transfers between devices with their start and end apart: 44, of which 27 were waited for; matrix products, arithmetic and copies ran while one was open for 1% of the time, Pallas kernels for 2%

profile of v2, /device:TPU:24, one launch (start us, length us, event | category | flops | bytes accessed | tf_op | source)
XLA Modules:
  0.0 144.5 jit_solution(4572731818879612850)
XLA Ops:
  0.6 2.0 %collective-permute-start.44 = (bf16[128,896]{1,0:T(8,128)(2,1)}, bf16[128,896]{1,0:T(8,128)(2,1)S(1)}, u32[]{:S(2)}, u32[]{:S(2)}) collective-permute-start(bf16[128,896]{1,0:T(8,128)(2,1)} %refs_0_.3), channel_id=1, source_target_pairs={{0,8},{8,16},{16,24},{24,32},{32,40},{40,48},{48,56},{56,0},{1,9},... | collective-permute-start | bytes 688136 | tf_op jit(solution)/shard_map/gather/ppermute | solution.py:358
  2.6 4.0 %collective-permute-start.45 = (bf16[128,896]{1,0:T(8,128)(2,1)}, bf16[128,896]{1,0:T(8,128)(2,1)S(1)}, u32[]{:S(2)}, u32[]{:S(2)}) collective-permute-start(bf16[128,896]{1,0:T(8,128)(2,1)} %refs_0_.3), channel_id=1, source_target_pairs={{0,56},{8,0},{16,8},{24,16},{32,24},{40,32},{48,40},{56,48},{1,57}... | collective-permute-start | bytes 688136 | tf_op jit(solution)/shard_map/gather/ppermute | solution.py:358
  6.7 2.1 %block_list.3 = (s32[3,88]{1,0:T(4,128)S(1)}, s32[1]{0:T(128)}) custom-call(s32[4,64]{1,0:T(4,128)} %bitcast.15, s32[64]{0:T(128)} %count_ref.1, s32[4,64]{1,0:T(4,128)} %bitcast.16, s32[1,64]{1,0:T(1,128)} %bitcast.19), custom_call_target="tpu_custom_call" | custom-call | tf_op jit(solution)/shard_map/block_list/pallas_call | solution.py:100
  8.7 3.6 %collective-permute-done.44.refs_4_ = bf16[128,896]{1,0:T(8,128)(2,1)S(1)} collective-permute-done((bf16[128,896]{1,0:T(8,128)(2,1)}, bf16[128,896]{1,0:T(8,128)(2,1)S(1)}, u32[]{:S(2)}, u32[]{:S(2)}) %collective-permute-start.44) | collective-permute-done | bytes 229408 | tf_op jit(solution)/shard_map/gather/ppermute | solution.py:358
  12.4 3.2 %collective-permute-start.46 = (bf16[128,896]{1,0:T(8,128)(2,1)S(1)}, bf16[128,896]{1,0:T(8,128)(2,1)S(1)}, u32[]{:S(2)}, u32[]{:S(2)}) collective-permute-start(bf16[128,896]{1,0:T(8,128)(2,1)S(1)} %collective-permute-done.45.refs_1_), channel_id=1, source_target_pairs={{0,56},{8,0},{16,8},{24,16},{32,24},{40,32},{48,40},{56,48},{1,57}... | collective-permute-start | bytes 688136 | tf_op jit(solution)/shard_map/gather/ppermute | solution.py:358
  17.3 2.2 %collective-permute-start.57 = (bf16[128,896]{1,0:T(8,128)(2,1)}, bf16[128,896]{1,0:T(8,128)(2,1)S(1)}, u32[]{:S(2)}, u32[]{:S(2)}) collective-permute-start(bf16[128,896]{1,0:T(8,128)(2,1)} %refs_9_.3), channel_id=1, source_target_pairs={{0,64},{64,128},{128,192},{192,0},{1,65},{65,129},{129,193},{193,1... | collective-permute-start | bytes 688136 | tf_op jit(solution)/shard_map/gather/ppermute | solution.py:358
  20.4 3.2 %collective-permute-start.47 = (bf16[128,896]{1,0:T(8,128)(2,1)S(1)}, bf16[128,896]{1,0:T(8,128)(2,1)S(1)}, u32[]{:S(2)}, u32[]{:S(2)}) collective-permute-start(bf16[128,896]{1,0:T(8,128)(2,1)S(1)} %collective-permute-done.46.refs_2_), channel_id=1, source_target_pairs={{0,56},{8,0},{16,8},{24,16},{32,24},{40,32},{48,40},{56,48},{1,57}... | collective-permute-start | bytes 688136 | tf_op jit(solution)/shard_map/gather/ppermute | solution.py:358
  23.6 4.6 %collective-permute-done.53.refs_11_ = bf16[128,896]{1,0:T(8,128)(2,1)S(1)} collective-permute-done((bf16[128,896]{1,0:T(8,128)(2,1)}, bf16[128,896]{1,0:T(8,128)(2,1)S(1)}, u32[]{:S(2)}, u32[]{:S(2)}) %collective-permute-start.53) | collective-permute-done | bytes 229408 | tf_op jit(solution)/shard_map/gather/ppermute | solution.py:358
  30.1 2.5 %collective-permute-start.51 = (bf16[64,896]{1,0:T(8,128)(2,1)S(1)}, bf16[64,896]{1,0:T(8,128)(2,1)S(1)}, u32[]{:S(2)}, u32[]{:S(2)}) collective-permute-start(bf16[64,896]{1,0:T(8,128)(2,1)S(1)} %slice.25), channel_id=1, source_target_pairs={{0,56},{8,0},{16,8},{24,16},{32,24},{40,32},{48,40},{56,48},{1,57}... | collective-permute-start | bytes 344072 | tf_op jit(solution)/shard_map/gather/ppermute | solution.py:358
  32.7 3.0 %collective-permute-done.50.refs_7_ = bf16[64,896]{1,0:T(8,128)(2,1)S(1)} collective-permute-done((bf16[64,896]{1,0:T(8,128)(2,1)S(1)}, bf16[64,896]{1,0:T(8,128)(2,1)S(1)}, u32[]{:S(2)}, u32[]{:S(2)}) %collective-permute-start.50) | collective-permute-done | bytes 114720 | tf_op jit(solution)/shard_map/gather/ppermute | solution.py:358
  35.7 2.3 %scores.3 = (f32[18,32,128]{2,1,0:T(8,128)S(1)}, f32[18,32,128]{2,1,0:T(8,128)S(1)}, f32[18,32,128]{2,1,0:T(8,128)S(1)}, f32[18,32,128]{2,1,0:T(8,128)S(1)}) custom-call(s32[3,88]{1,0:T(4,128)S(1)} %get-tuple-element.119.ent, bf16[128,896]{1,0:T(8,128)(2,1)} %refs_0_.3, bf16[128,896]{1,0:T(8,128)(2,1)S(1)} %collective-permute-done.45.refs_1_, ...), custom_call_target="tpu_custom_call" | custom-call | tf_op jit(solution)/shard_map/scores/pallas_call | solution.py:169
  39.6 2.7 %collective-permute-start.60 = (f32[18,32,128]{2,1,0:T(8,128)S(1)}, f32[18,32,128]{2,1,0:T(8,128)S(1)}, u32[]{:S(2)}, u32[]{:S(2)}) collective-permute-start(f32[18,32,128]{2,1,0:T(8,128)S(1)} %get-tuple-element.124), channel_id=1, source_target_pairs={{0,2},{1,3},{2,0},{3,1},{4,6},{5,7},{6,4},{7,5},{8,10},{9,11},{10,... | collective-permute-start | bytes 884744 | tf_op jit(solution)/shard_map/scores_over_x/ppermute | solution.py:358
  43.8 4.5 %collective-permute-done.59.s1 = f32[18,32,128]{2,1,0:T(8,128)S(1)} collective-permute-done((f32[18,32,128]{2,1,0:T(8,128)S(1)}, f32[18,32,128]{2,1,0:T(8,128)S(1)}, u32[]{:S(2)}, u32[]{:S(2)}) %collective-permute-start.59) | collective-permute-done | bytes 294944 | tf_op jit(solution)/shard_map/scores_over_x/ppermute | solution.py:358
  48.3 6.7 %collective-permute-done.60.s2 = f32[18,32,128]{2,1,0:T(8,128)S(1)} collective-permute-done((f32[18,32,128]{2,1,0:T(8,128)S(1)}, f32[18,32,128]{2,1,0:T(8,128)S(1)}, u32[]{:S(2)}, u32[]{:S(2)}) %collective-permute-start.60) | collective-permute-done | bytes 294944 | tf_op jit(solution)/shard_map/scores_over_x/ppermute | solution.py:358
  56.0 2.5 %collective-permute-start.62 = (f32[18,32,128]{2,1,0:T(8,128)S(1)}, f32[18,32,128]{2,1,0:T(8,128)S(1)}, u32[]{:S(2)}, u32[]{:S(2)}) collective-permute-start(f32[18,32,128]{2,1,0:T(8,128)S(1)} %get-tuple-element.126.refs_0_), channel_id=1, source_target_pairs={{0,3},{1,0},{2,1},{3,2},{4,7},{5,4},{6,5},{7,6},{8,11},{9,8},{10,9... | collective-permute-start | bytes 884744 | tf_op jit(solution)/shard_map/stats/ppermute | solution.py:358
  60.5 2.9 %collective-permute-start.66 = (f32[2,32,128]{2,1,0:T(8,128)S(1)}, f32[2,32,128]{2,1,0:T(8,128)S(1)}, u32[]{:S(2)}, u32[]{:S(2)}) collective-permute-start(f32[2,32,128]{2,1,0:T(8,128)S(1)} %get-tuple-element.127.refs_0_), channel_id=1, source_target_pairs={{0,56},{8,0},{16,8},{24,16},{32,24},{40,32},{48,40},{56,48},{1,57}... | collective-permute-start | bytes 98312 | tf_op jit(solution)/shard_map/stats/ppermute | solution.py:358
  63.4 1.9 %collective-permute-done.65.refs_1_ = f32[2,32,128]{2,1,0:T(8,128)S(1)} collective-permute-done((f32[2,32,128]{2,1,0:T(8,128)S(1)}, f32[2,32,128]{2,1,0:T(8,128)S(1)}, u32[]{:S(2)}, u32[]{:S(2)}) %collective-permute-start.65) | collective-permute-done | bytes 32800 | tf_op jit(solution)/shard_map/stats/ppermute | solution.py:358
  66.5 4.2 %collective-permute-start.68 = (f32[2,32,128]{2,1,0:T(8,128)S(1)}, f32[2,32,128]{2,1,0:T(8,128)S(1)}, u32[]{:S(2)}, u32[]{:S(2)}) collective-permute-start(f32[2,32,128]{2,1,0:T(8,128)S(1)} %get-tuple-element.128.refs_0_), channel_id=1, source_target_pairs={{0,24},{8,32},{16,40},{24,48},{32,56},{40,0},{48,8},{56,16},{1,25}... | collective-permute-start | bytes 98312 | tf_op jit(solution)/shard_map/stats/ppermute | solution.py:358
  71.6 2.5 %collective-permute-done.68.refs_2_ = f32[2,32,128]{2,1,0:T(8,128)S(1)} collective-permute-done((f32[2,32,128]{2,1,0:T(8,128)S(1)}, f32[2,32,128]{2,1,0:T(8,128)S(1)}, u32[]{:S(2)}, u32[]{:S(2)}) %collective-permute-start.68) | collective-permute-done | bytes 32800 | tf_op jit(solution)/shard_map/stats/ppermute | solution.py:358
  76.8 2.2 %collective-permute-start.71 = (f32[2,32,128]{2,1,0:T(8,128)S(1)}, f32[2,32,128]{2,1,0:T(8,128)S(1)}, u32[]{:S(2)}, u32[]{:S(2)}) collective-permute-start(f32[2,32,128]{2,1,0:T(8,128)S(1)} %get-tuple-element.129.refs_1_), channel_id=1, source_target_pairs={{0,128},{64,192},{128,0},{192,64},{1,129},{65,193},{129,1},{193,65... | collective-permute-start | bytes 98312 | tf_op jit(solution)/shard_map/stats/ppermute | solution.py:358
  79.4 2.0 %collective-permute-start.72 = (f32[2,32,128]{2,1,0:T(8,128)S(1)}, f32[2,32,128]{2,1,0:T(8,128)S(1)}, u32[]{:S(2)}, u32[]{:S(2)}) collective-permute-start(f32[2,32,128]{2,1,0:T(8,128)S(1)} %get-tuple-element.129.refs_1_), channel_id=1, source_target_pairs={{0,64},{64,128},{128,192},{192,0},{1,65},{65,129},{129,193},{193,1... | collective-permute-start | bytes 98312 | tf_op jit(solution)/shard_map/stats/ppermute | solution.py:358
  83.4 2.8 %collective-permute-start.73 = (f32[2,32,128]{2,1,0:T(8,128)S(1)}, f32[2,32,128]{2,1,0:T(8,128)S(1)}, u32[]{:S(2)}, u32[]{:S(2)}) collective-permute-start(f32[2,32,128]{2,1,0:T(8,128)S(1)} %final_stats.3.refs_4_), channel_id=1, source_target_pairs={{0,3},{1,0},{2,1},{3,2},{4,7},{5,4},{6,5},{7,6},{8,11},{9,8},{10,9... | collective-permute-start | bytes 98312 | tf_op jit(solution)/shard_map/stats/ppermute | solution.py:358
  89.2 2.4 %collective-permute-done.74.refs_6_ = f32[2,32,128]{2,1,0:T(8,128)S(1)} collective-permute-done((f32[2,32,128]{2,1,0:T(8,128)S(1)}, f32[2,32,128]{2,1,0:T(8,128)S(1)}, u32[]{:S(2)}, u32[]{:S(2)}) %collective-permute-start.74) | collective-permute-done | bytes 32800 | tf_op jit(solution)/shard_map/stats/ppermute | solution.py:358
  93.3 3.2 %query_grads.3 = (bf16[18,128,128]{2,1,0:T(8,128)(2,1)S(1)}, f32[128,896]{1,0:T(8,128)S(1)}, bf16[128,896]{1,0:T(8,128)(2,1)S(1)}, bf16[128,896]{1,0:T(8,128)(2,...) custom-call(s32[3,88]{1,0:T(4,128)S(1)} %get-tuple-element.119.ent, ...), custom_call_target="tpu_custom_call" | custom-call | flops 1000000000 | bytes 12000000 | tf_op jit(solution)/shard_map/query_grads/pallas_call | solution.py:293
  96.5 2.5 %code_grads.3 = (f32[128,896]{1,0:T(8,128)S(1)}, bf16[128,896]{1,0:T(8,128)(2,1)S(1)}, bf16[128,896]{1,0:T(8,128)(2,1)S(1)}, bf16[128,896]{1,0:T(8,128)(2,1)S(1)}, bf16[4,128,896]{2,1,0:T(8,128)(2,1)S(1)}) custom-call(s32[3,88]{1,0:T(4,128)S(1)} %get-tuple-element.119.ent, bf16[18,128,128]{2,1,0:T(8,128)(2,1)S(1)} %get-tuple-element.146.g_ref, ...), custom_call_target="tpu_custom_call" | custom-call | flops 1000000000 | bytes 12000000 | tf_op jit(solution)/shard_map/code_grads/pallas_call | solution.py:340
  99.1 2.7 %collective-permute-start.76 = (bf16[64,896]{1,0:T(8,128)(2,1)S(1)}, bf16[64,896]{1,0:T(8,128)(2,1)S(1)}, u32[]{:S(2)}, u32[]{:S(2)}) collective-permute-start(bf16[64,896]{1,0:T(8,128)(2,1)S(1)} %get-tuple-element.132), channel_id=1, source_target_pairs={{0,8},{8,16},{16,24},{24,32},{32,40},{40,48},{48,56},{56,0},{1,9},... | collective-permute-start | bytes 344072 | tf_op jit(solution)/shard_map/reduce/ppermute | solution.py:358
  102.6 3.6 %collective-permute-done.76.refs_0_ = bf16[64,896]{1,0:T(8,128)(2,1)S(1)} collective-permute-done((bf16[64,896]{1,0:T(8,128)(2,1)S(1)}, bf16[64,896]{1,0:T(8,128)(2,1)S(1)}, u32[]{:S(2)}, u32[]{:S(2)}) %collective-permute-start.76) | collective-permute-done | bytes 114720 | tf_op jit(solution)/shard_map/reduce/ppermute | solution.py:358
  110.4 4.8 %collective-permute-done.78.refs_0_ = bf16[128,896]{1,0:T(8,128)(2,1)S(1)} collective-permute-done((bf16[128,896]{1,0:T(8,128)(2,1)S(1)}, bf16[128,896]{1,0:T(8,128)(2,1)S(1)}, u32[]{:S(2)}, u32[]{:S(2)}) %collective-permute-start.78) | collective-permute-done | bytes 229408 | tf_op jit(solution)/shard_map/reduce/ppermute | solution.py:358
  119.3 4.0 %collective-permute-done.80.refs_0_ = bf16[128,896]{1,0:T(8,128)(2,1)S(1)} collective-permute-done((bf16[128,896]{1,0:T(8,128)(2,1)S(1)}, bf16[128,896]{1,0:T(8,128)(2,1)S(1)}, u32[]{:S(2)}, u32[]{:S(2)}) %collective-permute-start.80) | collective-permute-done | bytes 229408 | tf_op jit(solution)/shard_map/reduce/ppermute | solution.py:358
  127.1 4.8 %collective-permute-start.85 = (bf16[128,896]{1,0:T(8,128)(2,1)S(1)}, bf16[128,896]{1,0:T(8,128)(2,1)S(1)}, u32[]{:S(2)}, u32[]{:S(2)}) collective-permute-start(bf16[128,896]{1,0:T(8,128)(2,1)S(1)} %get-tuple-element.152), channel_id=1, source_target_pairs={{0,64},{64,128},{128,192},{192,0},{1,65},{65,129},{129,193},{193,1... | collective-permute-start | bytes 688136 | tf_op jit(solution)/shard_map/reduce/ppermute | solution.py:358
  133.8 5.4 %collective-permute-done.85 = bf16[128,896]{1,0:T(8,128)(2,1)S(1)} collective-permute-done((bf16[128,896]{1,0:T(8,128)(2,1)S(1)}, bf16[128,896]{1,0:T(8,128)(2,1)S(1)}, u32[]{:S(2)}, u32[]{:S(2)}) %collective-permute-start.85) | collective-permute-done | bytes 229408 | tf_op jit(solution)/shard_map/reduce/ppermute | solution.py:358
  140.5 2.0 %collective-permute-done.87 = bf16[128,896]{1,0:T(8,128)(2,1)S(1)} collective-permute-done((bf16[128,896]{1,0:T(8,128)(2,1)S(1)}, bf16[128,896]{1,0:T(8,128)(2,1)S(1)}, u32[]{:S(2)}, u32[]{:S(2)}) %collective-permute-start.87) | collective-permute-done | bytes 229408 | tf_op jit(solution)/shard_map/reduce/ppermute | solution.py:358
  (78 shorter events, 40.2 us)
Async XLA Ops:
  0.6 11.7 %collective-permute-start.44 = (bf16[128,896]{1,0:T(8,128)(2,1)}, bf16[128,896]{1,0:T(8,128)(2,1)S(1)}, u32[]{:S(2)}, u32[]{:S(2)}) collective-permute-start(bf16[128,896]{1,0:T(8,128)(2,1)} %refs_0_.3), channel_id=1, source_target_pairs={{0,8},{8,16},{16,24},{24,32},{32,40},{40,48},{48,56},{56,0},{1,9},... | collective-permute-start | bytes 688136 | tf_op jit(solution)/shard_map/gather/ppermute | solution.py:358
  2.6 9.8 %collective-permute-start.45 = (bf16[128,896]{1,0:T(8,128)(2,1)}, bf16[128,896]{1,0:T(8,128)(2,1)S(1)}, u32[]{:S(2)}, u32[]{:S(2)}) collective-permute-start(bf16[128,896]{1,0:T(8,128)(2,1)} %refs_0_.3), channel_id=1, source_target_pairs={{0,56},{8,0},{16,8},{24,16},{32,24},{40,32},{48,40},{56,48},{1,57}... | collective-permute-start | bytes 688136 | tf_op jit(solution)/shard_map/gather/ppermute | solution.py:358
  12.4 8.0 %collective-permute-start.48 = (bf16[128,896]{1,0:T(8,128)(2,1)S(1)}, bf16[128,896]{1,0:T(8,128)(2,1)S(1)}, u32[]{:S(2)}, u32[]{:S(2)}) collective-permute-start(bf16[128,896]{1,0:T(8,128)(2,1)S(1)} %collective-permute-done.44.refs_4_), channel_id=1, source_target_pairs={{0,8},{8,16},{16,24},{24,32},{32,40},{40,48},{48,56},{56,0},{1,9},... | collective-permute-start | bytes 688136 | tf_op jit(solution)/shard_map/gather/ppermute | solution.py:358
  12.4 8.0 %collective-permute-start.46 = (bf16[128,896]{1,0:T(8,128)(2,1)S(1)}, bf16[128,896]{1,0:T(8,128)(2,1)S(1)}, u32[]{:S(2)}, u32[]{:S(2)}) collective-permute-start(bf16[128,896]{1,0:T(8,128)(2,1)S(1)} %collective-permute-done.45.refs_1_), channel_id=1, source_target_pairs={{0,56},{8,0},{16,8},{24,16},{32,24},{40,32},{48,40},{56,48},{1,57}... | collective-permute-start | bytes 688136 | tf_op jit(solution)/shard_map/gather/ppermute | solution.py:358
  15.6 12.6 %collective-permute-start.53 = (bf16[128,896]{1,0:T(8,128)(2,1)}, bf16[128,896]{1,0:T(8,128)(2,1)S(1)}, u32[]{:S(2)}, u32[]{:S(2)}) collective-permute-start(bf16[128,896]{1,0:T(8,128)(2,1)} %refs_9_.3), channel_id=1, source_target_pairs={{0,192},{64,0},{128,64},{192,128},{1,193},{65,1},{129,65},{193,129... | collective-permute-start | bytes 688136 | tf_op jit(solution)/shard_map/gather/ppermute | solution.py:358
  16.4 11.8 %collective-permute-start.55 = (bf16[128,896]{1,0:T(8,128)(2,1)}, bf16[128,896]{1,0:T(8,128)(2,1)S(1)}, u32[]{:S(2)}, u32[]{:S(2)}) collective-permute-start(bf16[128,896]{1,0:T(8,128)(2,1)} %refs_9_.3), channel_id=1, source_target_pairs={{0,128},{64,192},{128,0},{192,64},{1,129},{65,193},{129,1},{193,65... | collective-permute-start | bytes 688136 | tf_op jit(solution)/shard_map/gather/ppermute | solution.py:358
  17.3 11.5 %collective-permute-start.57 = (bf16[128,896]{1,0:T(8,128)(2,1)}, bf16[128,896]{1,0:T(8,128)(2,1)S(1)}, u32[]{:S(2)}, u32[]{:S(2)}) collective-permute-start(bf16[128,896]{1,0:T(8,128)(2,1)} %refs_9_.3), channel_id=1, source_target_pairs={{0,64},{64,128},{128,192},{192,0},{1,65},{65,129},{129,193},{193,1... | collective-permute-start | bytes 688136 | tf_op jit(solution)/shard_map/gather/ppermute | solution.py:358
  20.4 8.4 %collective-permute-start.49 = (bf16[128,896]{1,0:T(8,128)(2,1)S(1)}, bf16[128,896]{1,0:T(8,128)(2,1)S(1)}, u32[]{:S(2)}, u32[]{:S(2)}) collective-permute-start(bf16[128,896]{1,0:T(8,128)(2,1)S(1)} %collective-permute-done.48.refs_5_), channel_id=1, source_target_pairs={{0,8},{8,16},{16,24},{24,32},{32,40},{40,48},{48,56},{56,0},{1,9},... | collective-permute-start | bytes 688136 | tf_op jit(solution)/shard_map/gather/ppermute | solution.py:358
  20.4 8.9 %collective-permute-start.47 = (bf16[128,896]{1,0:T(8,128)(2,1)S(1)}, bf16[128,896]{1,0:T(8,128)(2,1)S(1)}, u32[]{:S(2)}, u32[]{:S(2)}) collective-permute-start(bf16[128,896]{1,0:T(8,128)(2,1)S(1)} %collective-permute-done.46.refs_2_), channel_id=1, source_target_pairs={{0,56},{8,0},{16,8},{24,16},{32,24},{40,32},{48,40},{56,48},{1,57}... | collective-permute-start | bytes 688136 | tf_op jit(solution)/shard_map/gather/ppermute | solution.py:358
  29.4 6.4 %collective-permute-start.50 = (bf16[64,896]{1,0:T(8,128)(2,1)S(1)}, bf16[64,896]{1,0:T(8,128)(2,1)S(1)}, u32[]{:S(2)}, u32[]{:S(2)}) collective-permute-start(bf16[64,896]{1,0:T(8,128)(2,1)S(1)} %slice.24), channel_id=1, source_target_pairs={{0,8},{8,16},{16,24},{24,32},{32,40},{40,48},{48,56},{56,0},{1,9},... | collective-permute-start | bytes 344072 | tf_op jit(solution)/shard_map/gather/ppermute | solution.py:358
  30.1 5.6 %collective-permute-start.51 = (bf16[64,896]{1,0:T(8,128)(2,1)S(1)}, bf16[64,896]{1,0:T(8,128)(2,1)S(1)}, u32[]{:S(2)}, u32[]{:S(2)}) collective-permute-start(bf16[64,896]{1,0:T(8,128)(2,1)S(1)} %slice.25), channel_id=1, source_target_pairs={{0,56},{8,0},{16,8},{24,16},{32,24},{40,32},{48,40},{56,48},{1,57}... | collective-permute-start | bytes 344072 | tf_op jit(solution)/shard_map/gather/ppermute | solution.py:358
  38.1 10.2 %collective-permute-start.59 = (f32[18,32,128]{2,1,0:T(8,128)S(1)}, f32[18,32,128]{2,1,0:T(8,128)S(1)}, u32[]{:S(2)}, u32[]{:S(2)}) collective-permute-start(f32[18,32,128]{2,1,0:T(8,128)S(1)} %get-tuple-element.123), channel_id=1, source_target_pairs={{0,1},{1,2},{2,3},{3,0},{4,5},{5,6},{6,7},{7,4},{8,9},{9,10},{10,1... | collective-permute-start | bytes 884744 | tf_op jit(solution)/shard_map/scores_over_x/ppermute | solution.py:358
  39.6 15.4 %collective-permute-start.60 = (f32[18,32,128]{2,1,0:T(8,128)S(1)}, f32[18,32,128]{2,1,0:T(8,128)S(1)}, u32[]{:S(2)}, u32[]{:S(2)}) collective-permute-start(f32[18,32,128]{2,1,0:T(8,128)S(1)} %get-tuple-element.124), channel_id=1, source_target_pairs={{0,2},{1,3},{2,0},{3,1},{4,6},{5,7},{6,4},{7,5},{8,10},{9,11},{10,... | collective-permute-start | bytes 884744 | tf_op jit(solution)/shard_map/scores_over_x/ppermute | solution.py:358
  42.4 12.6 %collective-permute-start.61 = (f32[18,32,128]{2,1,0:T(8,128)S(1)}, f32[18,32,128]{2,1,0:T(8,128)S(1)}, u32[]{:S(2)}, u32[]{:S(2)}) collective-permute-start(f32[18,32,128]{2,1,0:T(8,128)S(1)} %get-tuple-element.125), channel_id=1, source_target_pairs={{0,3},{1,0},{2,1},{3,2},{4,7},{5,4},{6,5},{7,6},{8,11},{9,8},{10,9... | collective-permute-start | bytes 884744 | tf_op jit(solution)/shard_map/scores_over_x/ppermute | solution.py:358
  56.0 37.2 %collective-permute-start.62 = (f32[18,32,128]{2,1,0:T(8,128)S(1)}, f32[18,32,128]{2,1,0:T(8,128)S(1)}, u32[]{:S(2)}, u32[]{:S(2)}) collective-permute-start(f32[18,32,128]{2,1,0:T(8,128)S(1)} %get-tuple-element.126.refs_0_), channel_id=1, source_target_pairs={{0,3},{1,0},{2,1},{3,2},{4,7},{5,4},{6,5},{7,6},{8,11},{9,8},{10,9... | collective-permute-start | bytes 884744 | tf_op jit(solution)/shard_map/stats/ppermute | solution.py:358
  58.5 34.7 %collective-permute-start.63 = (f32[18,32,128]{2,1,0:T(8,128)S(1)}, f32[18,32,128]{2,1,0:T(8,128)S(1)}, u32[]{:S(2)}, u32[]{:S(2)}) collective-permute-start(f32[18,32,128]{2,1,0:T(8,128)S(1)} %get-tuple-element.126.refs_0_), channel_id=1, source_target_pairs={{0,2},{1,3},{2,0},{3,1},{4,6},{5,7},{6,4},{7,5},{8,10},{9,11},{10,... | collective-permute-start | bytes 884744 | tf_op jit(solution)/shard_map/stats/ppermute | solution.py:358
  59.7 33.6 %collective-permute-start.64 = (f32[18,32,128]{2,1,0:T(8,128)S(1)}, f32[18,32,128]{2,1,0:T(8,128)S(1)}, u32[]{:S(2)}, u32[]{:S(2)}) collective-permute-start(f32[18,32,128]{2,1,0:T(8,128)S(1)} %get-tuple-element.126.refs_0_), channel_id=1, source_target_pairs={{0,1},{1,2},{2,3},{3,0},{4,5},{5,6},{6,7},{7,4},{8,9},{9,10},{10,1... | collective-permute-start | bytes 884744 | tf_op jit(solution)/shard_map/stats/ppermute | solution.py:358
  66.5 7.6 %collective-permute-start.68 = (f32[2,32,128]{2,1,0:T(8,128)S(1)}, f32[2,32,128]{2,1,0:T(8,128)S(1)}, u32[]{:S(2)}, u32[]{:S(2)}) collective-permute-start(f32[2,32,128]{2,1,0:T(8,128)S(1)} %get-tuple-element.128.refs_0_), channel_id=1, source_target_pairs={{0,24},{8,32},{16,40},{24,48},{32,56},{40,0},{48,8},{56,16},{1,25}... | collective-permute-start | bytes 98312 | tf_op jit(solution)/shard_map/stats/ppermute | solution.py:358
  70.7 6.1 %collective-permute-start.69 = (f32[2,32,128]{2,1,0:T(8,128)S(1)}, f32[2,32,128]{2,1,0:T(8,128)S(1)}, u32[]{:S(2)}, u32[]{:S(2)}) collective-permute-start(f32[2,32,128]{2,1,0:T(8,128)S(1)} %get-tuple-element.130), channel_id=1, source_target_pairs={{0,40},{8,48},{16,56},{24,0},{32,8},{40,16},{48,24},{56,32},{1,41}... | collective-permute-start | bytes 98312 | tf_op jit(solution)/shard_map/stats/ppermute | solution.py:358
  76.8 5.4 %collective-permute-start.71 = (f32[2,32,128]{2,1,0:T(8,128)S(1)}, f32[2,32,128]{2,1,0:T(8,128)S(1)}, u32[]{:S(2)}, u32[]{:S(2)}) collective-permute-start(f32[2,32,128]{2,1,0:T(8,128)S(1)} %get-tuple-element.129.refs_1_), channel_id=1, source_target_pairs={{0,128},{64,192},{128,0},{192,64},{1,129},{65,193},{129,1},{193,65... | collective-permute-start | bytes 98312 | tf_op jit(solution)/shard_map/stats/ppermute | solution.py:358
  86.2 5.4 %collective-permute-start.74 = (f32[2,32,128]{2,1,0:T(8,128)S(1)}, f32[2,32,128]{2,1,0:T(8,128)S(1)}, u32[]{:S(2)}, u32[]{:S(2)}) collective-permute-start(f32[2,32,128]{2,1,0:T(8,128)S(1)} %final_stats.3.refs_4_), channel_id=1, source_target_pairs={{0,2},{1,3},{2,0},{3,1},{4,6},{5,7},{6,4},{7,5},{8,10},{9,11},{10,... | collective-permute-start | bytes 98312 | tf_op jit(solution)/shard_map/stats/ppermute | solution.py:358
  99.0 27.9 %collective-permute-start.84 = (bf16[4,128,896]{2,1,0:T(8,128)(2,1)S(1)}, bf16[4,128,896]{2,1,0:T(8,128)(2,1)S(1)}, u32[]{:S(2)}, u32[]{:S(2)}) collective-permute-start(bf16[4,128,896]{2,1,0:T(8,128)(2,1)S(1)} %get-tuple-element.148), channel_id=1, source_target_pairs={{0,4},{4,0},{1,5},{5,1},{2,6},{6,2},{3,7},{7,3},{8,12},{12,8},{9,1... | collective-permute-start | bytes 2752520 | tf_op jit(solution)/shard_map/reduce/ppermute | solution.py:358
  99.1 7.1 %collective-permute-start.76 = (bf16[64,896]{1,0:T(8,128)(2,1)S(1)}, bf16[64,896]{1,0:T(8,128)(2,1)S(1)}, u32[]{:S(2)}, u32[]{:S(2)}) collective-permute-start(bf16[64,896]{1,0:T(8,128)(2,1)S(1)} %get-tuple-element.132), channel_id=1, source_target_pairs={{0,8},{8,16},{16,24},{24,32},{32,40},{40,48},{48,56},{56,0},{1,9},... | collective-permute-start | bytes 344072 | tf_op jit(solution)/shard_map/reduce/ppermute | solution.py:358
  107.1 8.1 %collective-permute-start.78 = (bf16[128,896]{1,0:T(8,128)(2,1)S(1)}, bf16[128,896]{1,0:T(8,128)(2,1)S(1)}, u32[]{:S(2)}, u32[]{:S(2)}) collective-permute-start(bf16[128,896]{1,0:T(8,128)(2,1)S(1)} %get-tuple-element.136), channel_id=1, source_target_pairs={{0,8},{8,16},{16,24},{24,32},{32,40},{40,48},{48,56},{56,0},{1,9},... | collective-permute-start | bytes 688136 | tf_op jit(solution)/shard_map/reduce/ppermute | solution.py:358
  109.0 6.9 %collective-permute-start.79 = (bf16[128,896]{1,0:T(8,128)(2,1)S(1)}, bf16[128,896]{1,0:T(8,128)(2,1)S(1)}, u32[]{:S(2)}, u32[]{:S(2)}) collective-permute-start(bf16[128,896]{1,0:T(8,128)(2,1)S(1)} %get-tuple-element.137), channel_id=1, source_target_pairs={{0,56},{8,0},{16,8},{24,16},{32,24},{40,32},{48,40},{56,48},{1,57}... | collective-permute-start | bytes 688136 | tf_op jit(solution)/shard_map/reduce/ppermute | solution.py:358
  116.0 7.3 %collective-permute-start.80 = (bf16[128,896]{1,0:T(8,128)(2,1)S(1)}, bf16[128,896]{1,0:T(8,128)(2,1)S(1)}, u32[]{:S(2)}, u32[]{:S(2)}) collective-permute-start(bf16[128,896]{1,0:T(8,128)(2,1)S(1)} %get-tuple-element.140), channel_id=1, source_target_pairs={{0,8},{8,16},{16,24},{24,32},{32,40},{40,48},{48,56},{56,0},{1,9},... | collective-permute-start | bytes 688136 | tf_op jit(solution)/shard_map/reduce/ppermute | solution.py:358
  117.5 6.0 %collective-permute-start.81 = (bf16[128,896]{1,0:T(8,128)(2,1)S(1)}, bf16[128,896]{1,0:T(8,128)(2,1)S(1)}, u32[]{:S(2)}, u32[]{:S(2)}) collective-permute-start(bf16[128,896]{1,0:T(8,128)(2,1)S(1)} %get-tuple-element.141), channel_id=1, source_target_pairs={{0,56},{8,0},{16,8},{24,16},{32,24},{40,32},{48,40},{56,48},{1,57}... | collective-permute-start | bytes 688136 | tf_op jit(solution)/shard_map/reduce/ppermute | solution.py:358
  123.7 9.2 %collective-permute-start.82 = (bf16[128,896]{1,0:T(8,128)(2,1)S(1)}, bf16[128,896]{1,0:T(8,128)(2,1)S(1)}, u32[]{:S(2)}, u32[]{:S(2)}) collective-permute-start(bf16[128,896]{1,0:T(8,128)(2,1)S(1)} %get-tuple-element.144), channel_id=1, source_target_pairs={{0,8},{8,16},{16,24},{24,32},{32,40},{40,48},{48,56},{56,0},{1,9},... | collective-permute-start | bytes 688136 | tf_op jit(solution)/shard_map/reduce/ppermute | solution.py:358
  125.4 7.5 %collective-permute-start.83 = (bf16[128,896]{1,0:T(8,128)(2,1)S(1)}, bf16[128,896]{1,0:T(8,128)(2,1)S(1)}, u32[]{:S(2)}, u32[]{:S(2)}) collective-permute-start(bf16[128,896]{1,0:T(8,128)(2,1)S(1)} %get-tuple-element.145), channel_id=1, source_target_pairs={{0,56},{8,0},{16,8},{24,16},{32,24},{40,32},{48,40},{56,48},{1,57}... | collective-permute-start | bytes 688136 | tf_op jit(solution)/shard_map/reduce/ppermute | solution.py:358
  127.1 12.0 %collective-permute-start.85 = (bf16[128,896]{1,0:T(8,128)(2,1)S(1)}, bf16[128,896]{1,0:T(8,128)(2,1)S(1)}, u32[]{:S(2)}, u32[]{:S(2)}) collective-permute-start(bf16[128,896]{1,0:T(8,128)(2,1)S(1)} %get-tuple-element.152), channel_id=1, source_target_pairs={{0,64},{64,128},{128,192},{192,0},{1,65},{65,129},{129,193},{193,1... | collective-permute-start | bytes 688136 | tf_op jit(solution)/shard_map/reduce/ppermute | solution.py:358
  131.9 8.6 %collective-permute-start.86 = (bf16[128,896]{1,0:T(8,128)(2,1)S(1)}, bf16[128,896]{1,0:T(8,128)(2,1)S(1)}, u32[]{:S(2)}, u32[]{:S(2)}) collective-permute-start(bf16[128,896]{1,0:T(8,128)(2,1)S(1)} %get-tuple-element.153), channel_id=1, source_target_pairs={{0,128},{64,192},{128,0},{192,64},{1,129},{65,193},{129,1},{193,65... | collective-permute-start | bytes 688136 | tf_op jit(solution)/shard_map/reduce/ppermute | solution.py:358
  131.9 10.6 %collective-permute-start.87 = (bf16[128,896]{1,0:T(8,128)(2,1)S(1)}, bf16[128,896]{1,0:T(8,128)(2,1)S(1)}, u32[]{:S(2)}, u32[]{:S(2)}) collective-permute-start(bf16[128,896]{1,0:T(8,128)(2,1)S(1)} %get-tuple-element.154), channel_id=1, source_target_pairs={{0,192},{64,0},{128,64},{192,128},{1,193},{65,1},{129,65},{193,129... | collective-permute-start | bytes 688136 | tf_op jit(solution)/shard_map/reduce/ppermute | solution.py:358
  (15 other events, 125.9 us)
